TPU v7x, 256 devices: a whole 4x4x8 slice. The times are simulated.
256 devices in a mesh: expert: 64 (over y, z, core), etp: 4 (over x).
Axes of the slice: x: 4, y: 4, z: 8, core: 2. Of those that a mesh axis runs over, the one named last changes fastest.
Arguments:
- grad_out: bfloat16 [32768, 7168], P(('expert', 'etp')), may hold values from -1.5 to 1.5
- grad_exponent: int32 [32768, 56], P(('expert', 'etp')), may hold values from -2 to 1
- expert_ids: int32 [32768, 2], P(('expert', 'etp')), may hold values from 0 to 63, all different within a row; in each aligned block of 128 rows (0 to 127, 128 to 255, ...) at most 6 rows name the same one
- combine: bfloat16 [32768, 2], P(('expert', 'etp')), may hold values from 0.099609375 to 1
- saved_acts: bfloat16 [64, 4, 64, 6, 2, 1024], P('expert', 'etp'), may hold values from -6 to 6
- w_down: bfloat16 [64, 1024, 7168], P('expert', None, 'etp'), may hold values from -0.1875 to 0.1875
Outputs:
- pre_grad: bfloat16 [64, 4, 64, 6, 2, 1024], P('expert', 'etp')
- grad_down: bfloat16 [64, 1024, 7168], P('expert', None, 'etp')
- router_grad: float32 [32768, 2], P(('expert', 'etp'))
Inputs may be any that keep to these rules, and one draw needn't show every extreme that they name: `expert_ids`: in the rows of one device each expert is named at most 6 times, a bound that some block reaches; a token names 2 different experts.
All inputs are finite; a program needn't handle non-finite values.
Results may differ from a plain program's by a relative error of at most 0.0049.
Values may be sent and summed in bfloat16 or wider, within the bound.
A program may use at most 128 MiB of HBM per device.

v0:
```python
import jax
import jax.numpy as jnp
from jax import lax
from jax.sharding import PartitionSpec as P


def power_of_two(exponent):
    return jnp.where(
        exponent <= -2, 0.25, jnp.where(exponent == -1, 0.5, jnp.where(exponent == 0, 1.0, 2.0))
    ).astype(jnp.float32)


def backward_local(raw_grad, saved_rows, weight_rows):
    gate_pre = saved_rows[:, 0, :].astype(jnp.float32)
    up_pre = saved_rows[:, 1, :].astype(jnp.float32)
    sigmoid_gate = jax.nn.sigmoid(gate_pre)
    silu_gate = gate_pre * sigmoid_gate
    hidden = silu_gate * up_pre
    router_part = jnp.sum(hidden * raw_grad, axis=1)
    hidden_grad = weight_rows[:, None] * raw_grad
    grad_gate = hidden_grad * up_pre * (sigmoid_gate * (1.0 + gate_pre * (1.0 - sigmoid_gate)))
    grad_up = hidden_grad * silu_gate
    pre_grad = jnp.stack([grad_gate, grad_up], axis=1).astype(jnp.bfloat16)
    scaled = (weight_rows[:, None] * hidden).astype(jnp.bfloat16)
    return (pre_grad, scaled, router_part)


def local(grad_out, grad_exponent, expert_ids, combine, saved_acts, w_down):
    expert_count = lax.axis_size("expert")
    etp_count = lax.axis_size("etp")
    slot_cap = saved_acts.shape[3]
    tok_rows = grad_out.shape[0]
    feature_width = grad_out.shape[1]
    quarter_width = feature_width // etp_count
    block_count = grad_exponent.shape[1]
    route_count = expert_ids.shape[1]
    block_scale = power_of_two(grad_exponent)
    dequant = (
        (
            grad_out.astype(jnp.float32).reshape(
                tok_rows, block_count, feature_width // block_count
            )
            * block_scale[:, :, None]
        )
        .reshape(tok_rows, feature_width)
        .astype(jnp.bfloat16)
    )
    route_ids = expert_ids.reshape(-1)
    onehot = (route_ids[:, None] == jnp.arange(expert_count, dtype=jnp.int32)[None, :]).astype(
        jnp.int32
    )
    earlier = jnp.cumsum(onehot, axis=0) - onehot
    slot_index = jnp.sum(earlier * onehot, axis=1)
    target = route_ids * slot_cap + slot_index
    row_total = route_ids.shape[0]
    source_row = (
        jnp.full((expert_count * slot_cap,), -1, jnp.int32)
        .at[target]
        .set(jnp.arange(row_total, dtype=jnp.int32))
    )
    filled = source_row >= 0
    safe_row = jnp.maximum(source_row, 0)
    send_rows = jnp.where(
        filled[:, None], dequant[safe_row // route_count], jnp.zeros((), jnp.bfloat16)
    ).reshape(expert_count, slot_cap, feature_width)
    send_weights = jnp.where(
        filled, combine.reshape(-1)[safe_row], jnp.zeros((), jnp.bfloat16)
    ).reshape(expert_count, slot_cap)
    recv_rows, recv_weights = (
        lax.all_to_all(send_rows, "expert", split_axis=0, concat_axis=0, tiled=True),
        lax.all_to_all(send_weights, "expert", split_axis=0, concat_axis=0, tiled=True),
    )
    quarter_rows = lax.all_to_all(recv_rows[None], "etp", split_axis=3, concat_axis=0, tiled=True)
    own_slots = expert_count * slot_cap
    all_rows = quarter_rows.reshape(etp_count * own_slots, quarter_width)
    segment = all_rows
    raw_grad = lax.psum_scatter(
        lax.dot_general(
            segment, w_down[0], (((1,), (1,)), ((), ())), preferred_element_type=jnp.float32
        ),
        "etp",
        scatter_dimension=0,
        tiled=True,
    )
    saved_rows = saved_acts[0, 0].reshape(own_slots, 2, saved_acts.shape[5])
    pre_grad, scaled, router_part = backward_local(
        raw_grad, saved_rows, recv_weights.reshape(-1).astype(jnp.float32)
    )
    quarter_flat = quarter_rows.reshape(etp_count, own_slots, quarter_width)
    segment = quarter_flat
    grad_total = jnp.einsum(
        "krf,krd->fd",
        lax.all_gather(scaled[None], "etp", axis=0, tiled=True),
        segment,
        preferred_element_type=jnp.float32,
    )
    returned = lax.all_to_all(
        router_part.reshape(expert_count, slot_cap),
        "expert",
        split_axis=0,
        concat_axis=0,
        tiled=True,
    )
    router_grad = returned.reshape(-1)[target].reshape(tok_rows, route_count)
    return (pre_grad.reshape(saved_acts.shape), grad_total.astype(jnp.bfloat16)[None], router_grad)


def solution(mesh):
    placed = (
        P(("expert", "etp"), None),
        P(("expert", "etp"), None),
        P(("expert", "etp"), None),
        P(("expert", "etp"), None),
        P("expert", "etp", None, None, None, None),
        P("expert", None, "etp"),
    )
    return jax.shard_map(
        local,
        mesh=mesh,
        in_specs=placed,
        out_specs=(
            P("expert", "etp", None, None, None, None),
            P("expert", None, "etp"),
            P(("expert", "etp"), None),
        ),
        check_vma=False,
    )
```

profile of v0, /device:TPU:1, one launch (start us, length us, event | category | flops | bytes accessed | tf_op | source)
XLA Modules:
  0.0 496.7 jit_solution(11606334278221405803)
XLA Ops:
  7.2 0.8 copy.48
  8.3 0.7 broadcast_multiply_fusion
  9.0 0.6 reduce-window.6
  9.6 0.2 slice_reduce_fusion
  9.9 0.1 mul.97
  10.2 1.4 scatter_custom_fusion
  11.6 0.8 copy.51
  12.4 0.1 reshape.205
  12.6 2.7 gather_fusion
  15.3 0.1 broadcast_in_dim.59
  15.6 1.0 mul.100
  16.6 0.5 copy-done.2
  17.1 0.9 fusion.4
  17.9 6.5 %gather_fusion.1 = bf16[384,7168]{1,0:T(8,128)(2,1)} fusion(bf16[128,7168]{1,0:T(8,128)(2,1)S(1)} %fusion.4, s32[1024]{0:T(1024)S(1)} %get-tuple-element.22), kind=kCustom, calls=%fused_computation.1 | custom fusion | bytes 11011584 | tf_op jit(solution)/shard_map/gather | solution.py:64
  24.4 8.3 %gather.13 = bf16[64,6,7168]{2,1,0:T(8,128)(2,1)} reshape(bf16[384,7168]{1,0:T(8,128)(2,1)} %gather_fusion.1) | data formatting | bytes 11010048 | tf_op jit(solution)/shard_map/gather | solution.py:64
  32.8 3.8 broadcast_select_fusion
  36.6 176.4 %all_to_all.39 = bf16[64,6,7168]{2,1,0:T(8,128)(2,1)} all-to-all(bf16[64,6,7168]{2,1,0:T(8,128)(2,1)S(1)} %broadcast_select_fusion), channel_id=1, replica_groups=mesh['expert'=64,'etp'=4] {'expert'}, dimensions={0} | all-to-all | bytes 11010048 | tf_op jit(solution)/shard_map/all_to_all | solution.py:70
  213.1 19.3 %copy.54 = bf16[1,64,6,7168]{1,2,0,3:T(8,128)(2,1)} copy(bf16[1,64,6,7168]{3,2,1,0:T(8,128)(2,1)} %bitcast.117) | data formatting | bytes 11010048 | tf_op jit(solution)/shard_map/broadcast_in_dim | solution.py:73
  232.4 12.8 %reshape.267 = bf16[4,2,344064]{2,1,0:T(2,128)(2,1)} reshape(bf16[7168,1,6,64]{3,2,1,0:T(8,128)(2,1)} %bitcast.114) | data formatting | bytes 11010048
  245.2 68.8 %all_to_all.40 = bf16[4,2,344064]{2,1,0:T(2,128)(2,1)} all-to-all(bf16[4,2,344064]{2,1,0:T(2,128)(2,1)} %reshape.267), channel_id=1, replica_groups=mesh['expert'=64,'etp'=4] {'etp'}, dimensions={0} | all-to-all | bytes 11010048 | tf_op jit(solution)/shard_map/all_to_all | solution.py:73
  314.0 12.1 %reshape.268 = bf16[7168,1,6,64]{3,2,1,0:T(8,128)(2,1)} reshape(bf16[4,2,344064]{2,1,0:T(2,128)(2,1)} %all_to_all.40) | data formatting | bytes 11010048
  326.1 15.8 %copy.66 = bf16[1,64,6,4,1792]{4,3,1,2,0:T(4,128)(2,1)} copy(bf16[1,64,6,4,1792]{1,2,4,3,0:T(8,128)(2,1)} %bitcast.113) | data formatting | bytes 11010048 | tf_op jit(solution)/shard_map/all_to_all | solution.py:73
  341.9 8.6 %copy.56 = bf16[4,1,64,6,1792]{4,3,2,0,1:T(8,128)(2,1)} copy(bf16[4,1,64,6,1792]{4,0,2,3,1:T(4,128)(2,1)} %bitcast.115) | data formatting | bytes 11010048 | tf_op jit(solution)/shard_map/all_to_all | solution.py:73
  350.5 9.6 %reshape.206 = bf16[1536,1792]{1,0:T(8,128)(2,1)} reshape(bf16[4,1,64,6,1792]{4,3,2,0,1:T(8,128)(2,1)} %copy.56) | data formatting | bytes 11010048 | tf_op jit(solution)/shard_map/reshape | solution.py:75
  360.1 10.9 %fusion.5 = f32[1536,1024]{1,0:T(8,128)} fusion(bf16[1536,1792]{1,0:T(8,128)(2,1)} %reshape.206, bf16[1,1024,1792]{2,1,0:T(8,128)(2,1)} %param.11), kind=kOutput, calls=%fused_computation.10 | convolution fusion | flops 5637144576 | bytes 15466496 | tf_op jit(solution)/shard_map/dot_general | solution.py:78
  371.1 0.8 all_to_all.34
  371.9 6.7 %all-to-all-start = ((bf16[64,1,6]{2,1,0:T(2,128)(2,1)}), bf16[64,1,6]{2,1,0:T(2,128)(2,1)S(1)}, u32[]{:S(2)}, u32[]{:S(2)}) async-start(bf16[64,1,6]{2,1,0:T(2,128)(2,1)} %all_to_all.34), calls=%async_computation | async-start | bytes 65536 | tf_op jit(solution)/shard_map/all_to_all | solution.py:71
  378.6 0.3 all-gather.2.cloned.1.call-start
  378.9 3.1 fusion.39
  382.0 5.9 %all-to-all-done = bf16[64,1,6]{2,1,0:T(2,128)(2,1)S(1)} async-done(((bf16[64,1,6]{2,1,0:T(2,128)(2,1)}), bf16[64,1,6]{2,1,0:T(2,128)(2,1)S(1)}, u32[]{:S(2)}, u32[]{:S(2)}) %all-to-all-start) | async-done | bytes 800 | tf_op jit(solution)/shard_map/all_to_all | solution.py:71
  388.1 45.2 %reduce-scatter.2.cloned.1.call-done = f32[384,1024]{1,0:T(8,128)} async-done(((f32[1536,1024]{1,0:T(8,128)}), f32[384,1024]{1,0:T(8,128)}) %reduce-scatter.2.cloned.1.call-update) | async-done | bytes 1572880 | tf_op jit(solution)/shard_map/reduce_scatter | solution.py:77
  433.3 2.7 fusion.20
  436.0 1.4 fusion.23
  437.5 7.0 %copy.59 = bf16[4,1,64,6,1792]{4,0,3,2,1:T(4,128)(2,1)} copy(bf16[4,1,64,6,1792]{4,0,2,3,1:T(4,128)(2,1)} %bitcast.116) | data formatting | bytes 11010048 | tf_op jit(solution)/shard_map/all_to_all | solution.py:73
  444.5 1.8 fusion.18
  446.3 1.3 stack.10
  447.6 0.3 stack.9
  447.9 0.7 all_to_all.32
  448.7 10.6 %all-to-all-start.3 = ((f32[64,1,6]{2,1,0:T(1,128)}), f32[64,1,6]{2,1,0:T(1,128)S(1)}, u32[]{:S(2)}, u32[]{:S(2)}) async-start(f32[64,1,6]{2,1,0:T(1,128)} %bitcast.15), calls=%async_computation.4 | async-start | bytes 65536 | tf_op jit(solution)/shard_map/all_to_all | solution.py:97
  459.3 0.5 pad_maximum_fusion
  459.8 2.8 copy.63
  462.5 6.0 %all-to-all-done.3 = f32[64,1,6]{2,1,0:T(1,128)S(1)} async-done(((f32[64,1,6]{2,1,0:T(1,128)}), f32[64,1,6]{2,1,0:T(1,128)S(1)}, u32[]{:S(2)}, u32[]{:S(2)}) %all-to-all-start.3) | async-done | bytes 1568 | tf_op jit(solution)/shard_map/all_to_all | solution.py:97
  468.6 0.5 broadcast.135
  469.1 0.7 reduce.9
  470.0 1.9 gather_fusion.2
  472.1 0.6 copy.64
  472.7 6.7 %all-gather.2.cloned.1.call-done = bf16[4,384,1024]{2,1,0:T(8,128)(2,1)} async-done(((bf16[1,384,1024]{2,1,0:T(8,128)(2,1)}), bf16[4,384,1024]{2,1,0:T(8,128)(2,1)}) %all-gather.2.cloned.1.call-update) | async-done | bytes 3145744 | tf_op jit(solution)/shard_map/all_gather | solution.py:93
  479.4 10.5 %fusion.7 = bf16[1,1024,1792]{2,1,0:T(8,128)(2,1)} fusion(bf16[4,384,1024]{2,1,0:T(8,128)(2,1)} %all-gather.2.cloned.1.call-done, bf16[4,384,1792]{2,0,1:T(4,128)(2,1)} %bitcast.120), kind=kOutput, calls=%fused_computation.12 | convolution fusion | flops 5638979584 | bytes 12320768 | tf_op jit(solution)/shard_map/krf,krd->fd/dot_general | solution.py:91
  (29 shorter events, 1.3 us)
Async XLA Ops:
  7.2 8.3 %copy-start.3 = (s32[128,56]{0,1:T(8,128)S(1)}, s32[128,56]{0,1:T(8,128)}, u32[]{:S(2)}) copy-start(s32[128,56]{0,1:T(8,128)} %param.7) | copy-start | bytes 86020
  7.2 426.1 %reduce-scatter.2.cloned.1.call-start = ((), (), s32[]{:S(2)}) async-start(), calls=%async_computation.5 | async-start | bytes 7864320 | tf_op jit(solution)/shard_map/reduce_scatter | solution.py:77
  15.6 1.5 copy-start.2
  371.1 7.8 %copy-start = (bf16[1,1,64,6,2,1024]{5,4,3,2,1,0:T(2,128)(2,1)S(1)}, bf16[1,1,64,6,2,1024]{5,4,3,2,1,0:T(2,128)(2,1)}, u32[]{:S(2)}) copy-start(bf16[1,1,64,6,2,1024]{5,4,3,2,1,0:T(2,128)(2,1)} %param.10) | copy-start | bytes 4718596
  371.9 15.9 %all-to-all-start = ((bf16[64,1,6]{2,1,0:T(2,128)(2,1)}), bf16[64,1,6]{2,1,0:T(2,128)(2,1)S(1)}, u32[]{:S(2)}, u32[]{:S(2)}) async-start(bf16[64,1,6]{2,1,0:T(2,128)(2,1)} %all_to_all.34), calls=%async_computation | async-start | bytes 65536 | tf_op jit(solution)/shard_map/all_to_all | solution.py:71
  378.6 100.8 %all-gather.2.cloned.1.call-start = ((), (), s32[]{:S(2)}) async-start(), calls=%async_computation.6 | async-start | bytes 3932160 | tf_op jit(solution)/shard_map/all_gather | solution.py:93
  437.5 7.0 %copy-start.1 = (f32[384,1024]{1,0:T(8,128)S(1)}, f32[384,1024]{1,0:T(8,128)}, u32[]{:S(2)}) copy-start(f32[384,1024]{1,0:T(8,128)} %reduce-scatter.2.cloned.1.call-done) | copy-start | bytes 4718596
  448.7 19.9 %all-to-all-start.3 = ((f32[64,1,6]{2,1,0:T(1,128)}), f32[64,1,6]{2,1,0:T(1,128)S(1)}, u32[]{:S(2)}, u32[]{:S(2)}) async-start(f32[64,1,6]{2,1,0:T(1,128)} %bitcast.15), calls=%async_computation.4 | async-start | bytes 65536 | tf_op jit(solution)/shard_map/all_to_all | solution.py:97
Sparse Core Ops, SparseCore 0:
  371.2 62.0 reduce-scatter.1
  437.6 41.7 all-gather.1
where the time goes:
time: 499 us; the launch traced here: 497 us
  blocking collectives  245 us (49%)
  local copies, waits for them, and re-layouts  121 us (24%)
  waiting for transfers between devices  63.9 us (13%)
  matrix products  21.4 us (4%)
  starting transfers between devices  17.7 us (4%)
  between operations  14.3 us (3%)
  other arithmetic  13.4 us (3%)
    all_to_all x1, blocking collectives, local(): lax.all_to_all(send_rows, 'expert', split_axis=0, concat_axis=0, tiled=True)  176 us
    all_to_all x1, blocking collectives, local(): lax.all_to_all(recv_rows[None], 'etp', split_axis=3, concat_axis=0, tiled...  68.8 us
    reduce_scatter x1, waiting for transfers between devices, local(): lax.psum_scatter(lax.dot_general(segment, w_down[0], (((1,), (1,)), ((),...  45.2 us
    all_to_all x3, local copies, waits for them, and re-layouts, local(): lax.all_to_all(recv_rows[None], 'etp', split_axis=3, concat_axis=0, tiled...  31.4 us
    unnamed x14, local copies, waits for them, and re-layouts  30.4 us
    broadcast_in_dim x1, local copies, waits for them, and re-layouts, local(): recv_rows[None]  19.3 us
    gather x2, local copies, waits for them, and re-layouts, local(): dequant[safe_row // route_count]  14.8 us
    dot_general x1, matrix products, local(): lax.dot_general(segment, w_down[0], (((1,), (1,)), ((), ())), preferred_e...  10.9 us
  transfers between devices with their start and end apart: 4, of which 4 were waited for; matrix products, arithmetic and copies ran while one was open for 4% of the time, Pallas kernels for 0%

commit v1 on v0

v1 whole, which is shorter than its diff:
```python
import functools

import jax
import jax.numpy as jnp
import numpy as np
from jax import lax
from jax.experimental import pallas as pl
from jax.experimental.pallas import tpu as pltpu
from jax.sharding import PartitionSpec as P

MESH = pl.DeviceIdType.MESH
F32, BF16, I32 = jnp.float32, jnp.bfloat16, jnp.int32
NY, NZ, NC = 4, 8, 2
HALVES = 2


def power_of_two(exponent):
    return jnp.where(
        exponent <= -2, 0.25, jnp.where(exponent == -1, 0.5, jnp.where(exponent == 0, 1.0, 2.0))
    ).astype(F32)


def matmul(a, b):
    return jnp.dot(a, b, preferred_element_type=F32)


def constants(nx, cap, tok):
    gs = NY * NC
    rc = nx * cap
    own = gs * cap
    order = np.zeros((HALVES, gs * rc, gs * HALVES * rc), np.float32)
    for h in range(HALVES):
        for r in range(nx):
            for i in range(gs):
                for c in range(cap):
                    order[h, r * own + i * cap + c, (i * HALVES + h) * rc + r * cap + c] = 1
    split = np.zeros((2 * own, 2 * own), np.float32)
    for g in range(2):
        for j in range(own):
            split[g * own + j, 2 * j + g] = 1
    repeat = np.zeros((own, gs), np.float32)
    for j in range(own):
        repeat[j, j // cap] = 1
    pick = np.zeros((own, 128), np.float32)
    diag = np.zeros((own, 128), np.float32)
    for j in range(own):
        pick[j, j % cap] = 1
        diag[j, j] = 1
    before = np.triu(np.ones((tok, tok), np.float32), 1)
    bf = lambda a: jnp.asarray(a, BF16)
    return bf(order), bf(split), bf(split.T), bf(repeat), jnp.asarray(pick), jnp.asarray(diag), bf(before)


def kernel(
    nx, cap,
    grad_ref, exp_ref, ids_ref, comb_ref, saved_hbm, w_hbm,
    order_ref, split_ref, join_ref, repeat_ref, pick_ref, diag_ref, before_ref,
    pre_hbm, down_hbm, router_ref,
    xs, tok, ksend, krecv, keys, sbuf, rbuf, rows, w, sv, pstage, wsend, wrecv, wcol,
    scaled, scaled_all, scaled_t, pf, psend, precv, rrow, rrecv, down,
    in_sem, x_ssem, x_rsem, k_ssem, k_rsem, d_ssem, d_rsem, d_lsem, w_ssem, w_rsem,
    g_ssem, g_rsem, g_lsem, p_ssem, p_rsem, r_ssem, r_rsem, o_sem, o2_sem,
):
    me = lax.axis_index("expert")
    q = lax.axis_index("etp")
    y, z, core = me // (NZ * NC), (me // NC) % NZ, me % NC
    gs = NY * NC
    rc = nx * cap
    mr = HALVES * rc
    own = gs * cap
    ne = NY * NZ * NC
    tokens = grad_ref.shape[0]
    width = w.shape[1]
    half = width // HALVES
    blocks = exp_ref.shape[0]
    inner = [(dy, dc) for dy in range(NY) for dc in range(NC)]
    slot_me = y * NC + core

    def expert_of(dy, dz, dc):
        return ((y + dy) % NY) * (NZ * NC) + ((z + dz) % NZ) * NC + (core + dc) % NC

    def remote(src, dst, ssem, rsem, e, x):
        return pltpu.make_async_remote_copy(
            src_ref=src, dst_ref=dst, send_sem=ssem, recv_sem=rsem, device_id=(e, x), device_id_type=MESH
        )

    def plane_order(g):
        d = (g + 1) // 2
        return (NZ // 2 + d * (1 - 2 * (g % 2)) * -1 + NZ) % NZ

    w_in = pltpu.make_async_copy(w_hbm, w, in_sem.at[0])
    w_in.start()
    s_in = [pltpu.make_async_copy(saved_hbm.at[:, j], sv.at[j], in_sem.at[1 + j]) for j in range(NZ)]
    for c in s_in:
        c.start()

    bar = pltpu.get_barrier_semaphore()
    for d in range(1, nx):
        pl.semaphore_signal(bar, inc=1, device_id=(me, (q + d) % nx), device_id_type=MESH)

    def greet(k, _):
        pl.semaphore_signal(bar, inc=1, device_id=((me + k) % ne, q), device_id_type=MESH)
        return 0

    lax.fori_loop(1, ne, greet, 0)

    expert_iota = lax.broadcasted_iota(I32, (ne, tokens), 0)
    a = [jnp.where(expert_iota == ids_ref[k : k + 1, :], 1.0, 0.0) for k in range(2)]
    assigned = a[0] + a[1]
    slot = matmul(assigned.astype(BF16), before_ref[...])
    slot = jnp.where(assigned > 0, slot, -1.0)
    ksend[...] = slot
    combine = comb_ref[...].astype(F32)
    weight = a[0] * combine[0:1, :] + a[1] * combine[1:2, :]
    lane = lax.broadcasted_iota(I32, (ne, 128), 1)
    slot_weight = jnp.zeros((ne, 128), F32)
    for c in range(cap):
        total = jnp.sum(jnp.where(slot == c, weight, 0.0), axis=1, keepdims=True)
        slot_weight = jnp.where(lane == c, total, slot_weight)
    wsend[...] = slot_weight.reshape(ne, 1, 128)

    scale_t = power_of_two(exp_ref[...]).astype(BF16)
    blk = width // (width * nx // blocks)
    qb = width // blk
    block_iota = lax.broadcasted_iota(I32, (blocks, width), 0)
    col_block = lax.broadcasted_iota(I32, (blocks, width), 1) // qb
    for j in range(nx):
        expand = jnp.where(block_iota == col_block + j * blk, 1.0, 0.0).astype(BF16)
        scale = lax.dot_general(scale_t, expand, (((0,), (0,)), ((), ())), preferred_element_type=F32)
        deq = (grad_ref[:, j * width : (j + 1) * width].astype(F32) * scale).astype(BF16)
        for h in range(HALVES):
            xs[j, h] = deq[:, h * half : (h + 1) * half]

    pl.semaphore_wait(bar, ne - 1 + nx - 1)

    k_out, x_out = [], []
    for d in range(1, nx):
        p = (q + d) % nx
        k_out.append(remote(ksend, krecv.at[q], k_ssem.at[d - 1], k_rsem, me, p))
        k_out[-1].start()
    for d in range(1, nx):
        p = (q + d) % nx
        x_out.append(remote(xs.at[p], tok.at[:, q], x_ssem.at[d - 1], x_rsem, me, p))
        x_out[-1].start()
    x_own = pltpu.make_async_copy(xs.at[q], tok.at[:, q], in_sem.at[NZ + 1])
    x_own.start()
    krecv[q] = ksend[...]

    def send_weight(k, _):
        dz, rest = k // gs, k % gs
        dy, dc = rest // NC, rest % NC
        e = expert_of(dy, dz, dc)
        remote(wsend.at[e], wrecv.at[dz * gs + slot_me], w_ssem, w_rsem, e, q).start()
        return 0

    lax.fori_loop(1, ne, send_weight, 0)
    wrecv[slot_me] = wsend[me]

    remote(krecv.at[pl.ds(0, nx - 1)], krecv.at[pl.ds(0, nx - 1)], k_ssem.at[0], k_rsem, me, (q + 1) % nx).wait_recv()
    for r in range(nx):
        s = krecv[r]
        for h in range(HALVES):
            at = (h * nx + r) * tokens
            keys[:, at : at + tokens] = jnp.where(s >= 0, s + (h * rc + r * cap), -1.0)

    remote(tok.at[:, pl.ds(0, nx - 1)], tok.at[:, pl.ds(0, nx - 1)], x_ssem.at[0], x_rsem, me, (q + 1) % nx).wait_recv()
    x_own.wait()

    row_iota = lax.broadcasted_iota(I32, (mr, HALVES * nx * tokens), 0).astype(F32)

    def dispatch(g, _):
        dz = plane_order(g)
        for i in range(gs):
            e = (i // NC) * (NZ * NC) + ((z + dz) % NZ) * NC + i % NC
            hot = jnp.where(row_iota == keys[pl.ds(e, 1), :], 1.0, 0.0).astype(BF16)
            out = matmul(hot, tok[...].reshape(HALVES * nx * tokens, half))
            sbuf[dz, i * mr : (i + 1) * mr, :] = out.astype(BF16)

        def send(dy, dc):
            to = ((y + dy) % NY) * NC + (core + dc) % NC
            remote(
                sbuf.at[dz, pl.ds(pl.multiple_of(to * mr, mr), mr)],
                rbuf.at[dz, pl.ds(pl.multiple_of(slot_me * mr, mr), mr)],
                d_ssem.at[dz], d_rsem.at[dz], expert_of(dy, dz, dc), q,
            ).start()

        for dy, dc in inner:
            if (dy, dc) == (0, 0):
                @pl.when(dz != 0)
                def _():
                    send(0, 0)

                @pl.when(dz == 0)
                def _():
                    pltpu.make_async_copy(
                        sbuf.at[dz, pl.ds(pl.multiple_of(slot_me * mr, mr), mr)],
                        rbuf.at[dz, pl.ds(pl.multiple_of(slot_me * mr, mr), mr)],
                        d_lsem,
                    ).start()
            else:
                send(dy, dc)
        return 0

    lax.fori_loop(0, NZ, dispatch, 0)

    for c in s_in:
        c.wait()
    remote(wrecv.at[pl.ds(0, ne - 1)], wrecv.at[pl.ds(0, ne - 1)], w_ssem, w_rsem, me, (q + 1) % nx).wait_recv()

    def gate_up(dz):
        v = sv[(z - dz + NZ) % NZ].reshape(2 * own, w.shape[0])
        gu = matmul(split_ref[...], v)
        gate, up = gu[:own], gu[own:]
        sg = jax.nn.sigmoid(gate)
        return gate, up, sg, gate * sg

    def scale_hidden(dz, _):
        gate, up, sg, silu = gate_up(dz)
        wr = wrecv[pl.ds(dz * gs, gs)].reshape(gs, 128)
        col = jnp.sum(matmul(repeat_ref[...], wr.astype(BF16)) * pick_ref[...], axis=1, keepdims=True)
        wcol[dz] = jnp.broadcast_to(col, (own, 128))
        scaled[dz] = (col * (silu * up)).astype(BF16)
        return 0

    lax.fori_loop(0, NZ, scale_hidden, 0)
    g_out = []
    for d in range(1, nx):
        g_out.append(remote(scaled, scaled_all.at[:, q], g_ssem.at[d - 1], g_rsem, me, (q + d) % nx))
        g_out[-1].start()
    g_own = pltpu.make_async_copy(scaled, scaled_all.at[:, q], g_lsem)
    g_own.start()
    w_in.wait()
    remote(scaled_all.at[:, pl.ds(0, nx - 1)], scaled_all.at[:, pl.ds(0, nx - 1)], g_ssem.at[0], g_rsem, me, (q + 1) % nx).wait_recv()
    g_own.wait()
    ff = w.shape[0]
    flat_scaled = scaled_all.reshape(NZ * nx * own, ff)
    step = 256

    def turn(k, _):
        at = pl.multiple_of(k * step, step)
        scaled_t[:, pl.ds(at, step)] = flat_scaled[pl.ds(at, step), :].T
        return 0

    lax.fori_loop(0, NZ * nx * own // step, turn, 0)

    grp = nx * own

    def finish(g):
        dz = plane_order(g)
        zz = (z - dz + NZ) % NZ
        remote(precv.at[dz, pl.ds(0, nx - 1)], precv.at[dz, pl.ds(0, nx - 1)], p_ssem.at[dz], p_rsem.at[dz], me, (q + 1) % nx).wait_recv()
        raw = pf[g % 2, pl.ds(pl.multiple_of(q * own, own), own), :]
        for d in range(1, nx):
            raw = raw + precv[dz, (q + d) % nx].astype(F32)
        gate, up, sg, silu = gate_up(dz)
        part = jnp.sum(silu * up * raw, axis=1, keepdims=True)
        rrow[dz] = jnp.sum(part * diag_ref[...], axis=0, keepdims=True)
        for dy, dc in inner:
            e = (((y + dy) % NY) * NZ + zz) * NC + (core + dc) % NC

            def send():
                remote(rrow.at[dz], rrecv.at[me], r_ssem, r_rsem, e, q).start()

            if (dy, dc) == (0, 0):
                pl.when(dz != 0)(send)

                @pl.when(dz == 0)
                def _():
                    rrecv[me] = rrow[dz]
            else:
                send()
        hg = wcol[dz][:, 0:1] * raw
        g_gate = hg * up * (sg * (1.0 + gate * (1.0 - sg)))
        g_up = hg * silu
        both = jnp.concatenate([g_gate, g_up], axis=0).astype(BF16)
        pstage[zz] = matmul(join_ref[...], both).astype(BF16).reshape(pstage.shape[1:])
        pltpu.make_async_copy(pstage.at[zz], pre_hbm.at[:, zz], o_sem.at[zz]).start()

    def arrive(g, _):
        dz = plane_order(g)

        @pl.when(dz != 0)
        def _():
            remote(rbuf.at[dz], rbuf.at[dz], d_ssem.at[dz], d_rsem.at[dz], me, (q + 1) % nx).wait_recv()

        @pl.when(dz == 0)
        def _():
            part = rbuf.at[dz, pl.ds(0, (gs - 1) * mr)]
            remote(part, part, d_ssem.at[dz], d_rsem.at[dz], me, (q + 1) % nx).wait_recv()
            block = rbuf.at[dz, pl.ds(pl.multiple_of(slot_me * mr, mr), mr)]
            pltpu.make_async_copy(block, block, d_lsem).wait()

        at = pl.multiple_of(dz * grp, grp)
        for h in range(HALVES):
            rows[pl.ds(at, grp), h * half : (h + 1) * half] = matmul(order_ref[h], rbuf[dz]).astype(BF16)
        part = lax.dot_general(
            rows[pl.ds(at, grp), :], w[...], (((1,), (1,)), ((), ())), preferred_element_type=F32
        )
        pf[g % 2] = part
        psend[dz] = part.astype(BF16)
        for d in range(1, nx):
            p = (q + d) % nx
            remote(
                psend.at[dz, pl.ds(pl.multiple_of(p * own, own), own)], precv.at[dz, q],
                p_ssem.at[dz], p_rsem.at[dz], me, p,
            ).start()

        @pl.when(g > 0)
        def _():
            finish(g - 1)

        return 0

    lax.fori_loop(0, NZ, arrive, 0)

    def down_tile(k, _):
        at = pl.multiple_of(k * step, step)
        down[:, pl.ds(at, step)] = matmul(scaled_t[...], rows[:, pl.ds(at, step)]).astype(BF16)
        pltpu.make_async_copy(down.at[:, pl.ds(at, step)], down_hbm.at[:, pl.ds(at, step)], o2_sem.at[k]).start()
        return 0

    lax.fori_loop(0, width // step, down_tile, 0)
    finish(NZ - 1)

    remote(rrecv.at[pl.ds(0, ne - 1)], rrecv.at[pl.ds(0, ne - 1)], r_ssem, r_rsem, me, (q + 1) % nx).wait_recv()
    back = rrecv[...].reshape(ne, 128)
    value = jnp.zeros((ne, tokens), F32)
    for c in range(cap):
        column = jnp.sum(jnp.where(lane == slot_me * cap + c, back, 0.0), axis=1, keepdims=True)
        value = jnp.where(ksend[...] == c, column, value)
    for k in range(2):
        mine = jnp.where(expert_iota == ids_ref[k : k + 1, :], value, 0.0)
        router_ref[k : k + 1, :] = jnp.sum(mine, axis=0, keepdims=True)

    for c in k_out + x_out + g_out:
        c.wait_send()
    part = wsend.at[pl.ds(0, ne - 1)]
    remote(part, part, w_ssem, w_rsem, me, (q + 1) % nx).wait_send()
    part = rrecv.at[pl.ds(0, ne - 1)]
    remote(part, part, r_ssem, r_rsem, me, (q + 1) % nx).wait_send()
    for j in range(NZ):
        part = sbuf.at[j] if j else sbuf.at[j, pl.ds(0, (gs - 1) * mr)]
        remote(part, part, d_ssem.at[j], d_rsem.at[j], me, (q + 1) % nx).wait_send()
        part = psend.at[j, pl.ds(0, (nx - 1) * own)]
        remote(part, part, p_ssem.at[j], p_rsem.at[j], me, (q + 1) % nx).wait_send()
        pltpu.make_async_copy(pstage.at[j], pre_hbm.at[:, j], o_sem.at[j]).wait()
    for k in range(width // step):
        pltpu.make_async_copy(
            down.at[:, k * step : (k + 1) * step], down_hbm.at[:, k * step : (k + 1) * step], o2_sem.at[k]
        ).wait()


def local(grad_out, grad_exponent, expert_ids, combine, saved_acts, w_down):
    nx = lax.axis_size("etp")
    ne = NY * NZ * NC
    tokens, features = grad_out.shape
    cap, ff = saved_acts.shape[3], saved_acts.shape[5]
    width = features // nx
    half = width // HALVES
    gs = NY * NC
    own = gs * cap
    mr = HALVES * nx * cap
    consts = constants(nx, cap, tokens)
    vmem = pl.BlockSpec(memory_space=pltpu.VMEM)
    hbm = pl.BlockSpec(memory_space=pl.ANY)
    dma = pltpu.SemaphoreType.DMA
    saved = saved_acts.reshape(NY, NZ, NC * cap, 2, ff)
    pre, down, router = pl.pallas_call(
        functools.partial(kernel, nx, cap),
        out_shape=[
            jax.ShapeDtypeStruct(saved.shape, BF16),
            jax.ShapeDtypeStruct((ff, width), BF16),
            jax.ShapeDtypeStruct((2, tokens), F32),
        ],
        in_specs=[vmem] * 4 + [hbm] * 2 + [vmem] * len(consts),
        out_specs=[hbm, hbm, vmem],
        scratch_shapes=[
            pltpu.VMEM((nx, HALVES, tokens, half), BF16),
            pltpu.VMEM((HALVES, nx, tokens, half), BF16),
            pltpu.VMEM((ne, tokens), F32),
            pltpu.VMEM((nx, ne, tokens), F32),
            pltpu.VMEM((ne, HALVES * nx * tokens), F32),
            pltpu.VMEM((NZ, gs * mr, half), BF16),
            pltpu.VMEM((NZ, gs * mr, half), BF16),
            pltpu.VMEM((NZ * nx * own, width), BF16),
            pltpu.VMEM((ff, width), BF16),
            pltpu.VMEM((NZ, NY, NC * cap, 2, ff), BF16),
            pltpu.VMEM((NZ, NY, NC * cap, 2, ff), BF16),
            pltpu.VMEM((ne, 1, 128), F32),
            pltpu.VMEM((ne, 1, 128), F32),
            pltpu.VMEM((NZ, own, 128), F32),
            pltpu.VMEM((NZ, own, ff), BF16),
            pltpu.VMEM((NZ, nx, own, ff), BF16),
            pltpu.VMEM((ff, NZ * nx * own), BF16),
            pltpu.VMEM((2, nx * own, ff), F32),
            pltpu.VMEM((NZ, nx * own, ff), BF16),
            pltpu.VMEM((NZ, nx, own, ff), BF16),
            pltpu.VMEM((NZ, 1, 128), F32),
            pltpu.VMEM((ne, 1, 128), F32),
            pltpu.VMEM((ff, width), BF16),
            dma((NZ + 2,)),
            dma((nx - 1,)), dma,
            dma((nx - 1,)), dma,
            dma((NZ,)), dma((NZ,)), dma,
            dma, dma,
            dma((nx - 1,)), dma, dma,
            dma((NZ,)), dma((NZ,)),
            dma, dma,
            dma((NZ,)), dma((width // 256,)),
        ],
        compiler_params=pltpu.CompilerParams(
            collective_id=0, has_side_effects=True, vmem_limit_bytes=60 << 20
        ),
    )(grad_out, grad_exponent.T, expert_ids.T, combine.T, saved, w_down[0], *consts)
    return pre.reshape(saved_acts.shape), down[None], router.T


def solution(mesh):
    placed = (
        P(("expert", "etp"), None),
        P(("expert", "etp"), None),
        P(("expert", "etp"), None),
        P(("expert", "etp"), None),
        P("expert", "etp", None, None, None, None),
        P("expert", None, "etp"),
    )
    return jax.shard_map(
        local,
        mesh=mesh,
        in_specs=placed,
        out_specs=(
            P("expert", "etp", None, None, None, None),
            P("expert", None, "etp"),
            P(("expert", "etp"), None),
        ),
        check_vma=False,
    )
```

time: 499 us -> 203 us (0.41)
  blocking collectives: 245 us -> 0 us
  Pallas kernels: 0 us -> 193 us
  local copies, waits for them, and re-layouts: 121 us -> 8.31 us
  waiting for transfers between devices: 63.9 us -> 0 us
  matrix products: 21.4 us -> 0 us
  starting transfers between devices: 17.7 us -> 0 us
  between operations: 14.3 us -> 0.64 us
  other arithmetic: 13.4 us -> 0 us
    all_to_all x2 -> x0, blocking collectives: 245 us -> none  [the longest x1 176 us: local(): lax.all_to_all(send_rows, 'expert', split_axis=0, concat_axis=0, tiled=True)]
    pallas_call x0 -> x1, Pallas kernels: none -> 193 us  [local(): pl.pallas_call(functools.partial(kernel, nx, cap), out_shape=[jax.ShapeDt...]
    reduce_scatter x1 -> x0, waiting for transfers between devices: 45.2 us -> none  [local(): lax.psum_scatter(lax.dot_general(segment, w_down[0], (((1,), (1,)), ((),...]
    all_to_all x6 -> x0, local copies, waits for them, and re-layouts: 33.4 us -> none  [the longest x3 31.4 us: local(): lax.all_to_all(recv_rows[None], 'etp', split_axis=3, concat_axis=0, tiled...]
    unnamed x14 -> x5, local copies, waits for them, and re-layouts: 30.4 us -> 8.31 us
    dot_general x2 -> x0, matrix products: 21.4 us -> none  [the longest x1 10.9 us: local(): lax.dot_general(segment, w_down[0], (((1,), (1,)), ((), ())), preferred_e...]
    gather x4 -> x0, local copies, waits for them, and re-layouts: 19.5 us -> none  [the longest x2 14.8 us: local(): dequant[safe_row // route_count]]
    broadcast_in_dim x2 -> x0, local copies, waits for them, and re-layouts: 19.4 us -> none  [the longest x1 19.3 us: local(): recv_rows[None]]
  transfers between devices with their start and end apart: 4 -> 0, of which waited for: 4 -> 0; matrix products, arithmetic and copies ran while one was open for 4% -> 0% of each run, Pallas kernels for 0% -> 0%
where the time goes in v1:
time: 203 us; the launch traced here: 202 us
  Pallas kernels  193 us (95%)
  local copies, waits for them, and re-layouts  8.31 us (4%)
    pallas_call x1, Pallas kernels, local(): pl.pallas_call(functools.partial(kernel, nx, cap), out_shape=[jax.ShapeDt...  193 us
    unnamed x5, local copies, waits for them, and re-layouts  8.31 us

profile of v1, /device:TPU:1, one launch (start us, length us, event | category | flops | bytes accessed | tf_op | source)
XLA Modules:
  0.0 202.2 jit_solution(17375085558617700873)
XLA Ops:
  0.6 193.2 %shard_map.148 = (bf16[4,8,12,2,1024]{4,3,2,1,0:T(2,128)(2,1)}, bf16[1024,1792]{1,0:T(8,128)(2,1)}, f32[2,128]{1,0:T(2,128)}) custom-call(bf16[128,7168]{1,0:T(8,128)(2,1)} %grad_ref.1, s32[56,128]{1,0:T(8,128)} %bitcast.12, s32[2,128]{1,0:T(2,128)} %bitcast.13, bf16[2,128]{1,0:T(2,128)(2,1)} %bitcast.15, bf16[4,8,12,2,1024]{4,3,2,1,0:T(2,128)(2,1)} %bitcast.10, ...), custom_call_target="tpu_custom_call" | custom-call | tf_op jit(solution)/shard_map/pallas_call | solution.py:368
  193.9 3.6 %copy.19 = bf16[1,1,64,6,2,1024]{5,4,3,2,1,0:T(2,128)(2,1)} copy(bf16[1,1,64,6,2,1024]{5,4,3,2,1,0:T(2,128)(2,1)} %bitcast.11) | data formatting | bytes 3145728
  197.5 0.0 copy-start
  197.5 4.1 %copy.20 = bf16[1,1024,1792]{2,1,0:T(8,128)(2,1)} copy(bf16[1,1024,1792]{2,1,0:T(8,128)(2,1)} %bitcast.9) | data formatting | bytes 7340032
  201.6 0.0 copy-done
  201.6 0.6 copy.21
Async XLA Ops:
  197.5 4.1 %copy-start = (f32[2,128]{1,0:T(2,128)S(1)}, f32[2,128]{1,0:T(2,128)}, u32[]{:S(2)}) copy-start(f32[2,128]{1,0:T(2,128)} %get-tuple-element.8) | copy-start | bytes 3076

commit v2 on v1

--- a/solution.py
+++ b/solution.py
@@ -12,6 +12,7 @@
 F32, BF16, I32 = jnp.float32, jnp.bfloat16, jnp.int32
 NY, NZ, NC = 4, 8, 2
 HALVES = 2
+EARLY = 256
 
 
 def power_of_two(exponent):
@@ -57,7 +58,7 @@
     order_ref, split_ref, join_ref, repeat_ref, pick_ref, diag_ref, before_ref,
     pre_hbm, down_hbm, router_ref,
     xs, tok, ksend, krecv, keys, sbuf, rbuf, rows, w, sv, pstage, wsend, wrecv, wcol,
-    scaled, scaled_all, scaled_t, pf, psend, precv, rrow, rrecv, down,
+    scaled, scaled_all, scaled_t, pf, psend, precv, rrow, rrecv, acc, down,
     in_sem, x_ssem, x_rsem, k_ssem, k_rsem, d_ssem, d_rsem, d_lsem, w_ssem, w_rsem,
     g_ssem, g_rsem, g_lsem, p_ssem, p_rsem, r_ssem, r_rsem, o_sem, o2_sem,
 ):
@@ -84,9 +85,11 @@
             src_ref=src, dst_ref=dst, send_sem=ssem, recv_sem=rsem, device_id=(e, x), device_id_type=MESH
         )
 
-    def plane_order(g):
-        d = (g + 1) // 2
-        return (NZ // 2 + d * (1 - 2 * (g % 2)) * -1 + NZ) % NZ
+    def far_first(g):
+        return (NZ // 2 + ((g + 1) // 2) * (2 * (g % 2) - 1) + NZ) % NZ
+
+    def own_first(g):
+        return (NZ // 2 * ((g + NZ - 1) // NZ) + (g // 2) * (1 - 2 * (g % 2)) + NZ) % NZ
 
     w_in = pltpu.make_async_copy(w_hbm, w, in_sem.at[0])
     w_in.start()
@@ -138,10 +141,14 @@
         p = (q + d) % nx
         k_out.append(remote(ksend, krecv.at[q], k_ssem.at[d - 1], k_rsem, me, p))
         k_out[-1].start()
-    for d in range(1, nx):
-        p = (q + d) % nx
-        x_out.append(remote(xs.at[p], tok.at[:, q], x_ssem.at[d - 1], x_rsem, me, p))
-        x_out[-1].start()
+    cuts = [slice(0, EARLY), slice(EARLY, half)]
+    for part, cut in enumerate(cuts):
+        for d in range(1, nx):
+            p = (q + d) % nx
+            x_out.append(
+                remote(xs.at[p, :, :, cut], tok.at[:, q, :, cut], x_ssem.at[part, d - 1], x_rsem.at[part], me, p)
+            )
+            x_out[-1].start()
     x_own = pltpu.make_async_copy(xs.at[q], tok.at[:, q], in_sem.at[NZ + 1])
     x_own.start()
     krecv[q] = ksend[...]
@@ -163,24 +170,25 @@
             at = (h * nx + r) * tokens
             keys[:, at : at + tokens] = jnp.where(s >= 0, s + (h * rc + r * cap), -1.0)
 
-    remote(tok.at[:, pl.ds(0, nx - 1)], tok.at[:, pl.ds(0, nx - 1)], x_ssem.at[0], x_rsem, me, (q + 1) % nx).wait_recv()
     x_own.wait()
 
     row_iota = lax.broadcasted_iota(I32, (mr, HALVES * nx * tokens), 0).astype(F32)
 
-    def dispatch(g, _):
-        dz = plane_order(g)
+    def dispatch(part, order, g, _):
+        cut = cuts[part]
+        dz = order(g)
         for i in range(gs):
             e = (i // NC) * (NZ * NC) + ((z + dz) % NZ) * NC + i % NC
             hot = jnp.where(row_iota == keys[pl.ds(e, 1), :], 1.0, 0.0).astype(BF16)
-            out = matmul(hot, tok[...].reshape(HALVES * nx * tokens, half))
-            sbuf[dz, i * mr : (i + 1) * mr, :] = out.astype(BF16)
+            out = matmul(hot, tok[:, :, :, cut].reshape(HALVES * nx * tokens, cut.stop - cut.start))
+            sbuf[dz, i * mr : (i + 1) * mr, cut] = out.astype(BF16)
+
+        mine = pl.ds(pl.multiple_of(slot_me * mr, mr), mr)
 
         def send(dy, dc):
             to = ((y + dy) % NY) * NC + (core + dc) % NC
             remote(
-                sbuf.at[dz, pl.ds(pl.multiple_of(to * mr, mr), mr)],
-                rbuf.at[dz, pl.ds(pl.multiple_of(slot_me * mr, mr), mr)],
+                sbuf.at[dz, pl.ds(pl.multiple_of(to * mr, mr), mr), cut], rbuf.at[dz, mine, cut],
                 d_ssem.at[dz], d_rsem.at[dz], expert_of(dy, dz, dc), q,
             ).start()
 
@@ -192,16 +200,16 @@
 
                 @pl.when(dz == 0)
                 def _():
-                    pltpu.make_async_copy(
-                        sbuf.at[dz, pl.ds(pl.multiple_of(slot_me * mr, mr), mr)],
-                        rbuf.at[dz, pl.ds(pl.multiple_of(slot_me * mr, mr), mr)],
-                        d_lsem,
-                    ).start()
+                    pltpu.make_async_copy(sbuf.at[dz, mine, cut], rbuf.at[dz, mine, cut], d_lsem).start()
             else:
                 send(dy, dc)
         return 0
 
-    lax.fori_loop(0, NZ, dispatch, 0)
+    for part, order in enumerate((far_first, own_first)):
+        cut = cuts[part]
+        landed = tok.at[:, pl.ds(0, nx - 1), :, cut]
+        remote(landed, landed, x_ssem.at[part, 0], x_rsem.at[part], me, (q + 1) % nx).wait_recv()
+        lax.fori_loop(0, NZ, functools.partial(dispatch, part, order), 0)
 
     for c in s_in:
         c.wait()
@@ -214,12 +222,13 @@
         sg = jax.nn.sigmoid(gate)
         return gate, up, sg, gate * sg
 
-    def scale_hidden(dz, _):
+    def scale_hidden(g, _):
+        dz = own_first(g)
         gate, up, sg, silu = gate_up(dz)
         wr = wrecv[pl.ds(dz * gs, gs)].reshape(gs, 128)
         col = jnp.sum(matmul(repeat_ref[...], wr.astype(BF16)) * pick_ref[...], axis=1, keepdims=True)
-        wcol[dz] = jnp.broadcast_to(col, (own, 128))
-        scaled[dz] = (col * (silu * up)).astype(BF16)
+        wcol[g] = jnp.broadcast_to(col, (own, 128))
+        scaled[g] = (col * (silu * up)).astype(BF16)
         return 0
 
     lax.fori_loop(0, NZ, scale_hidden, 0)
@@ -230,25 +239,30 @@
     g_own = pltpu.make_async_copy(scaled, scaled_all.at[:, q], g_lsem)
     g_own.start()
     w_in.wait()
-    remote(scaled_all.at[:, pl.ds(0, nx - 1)], scaled_all.at[:, pl.ds(0, nx - 1)], g_ssem.at[0], g_rsem, me, (q + 1) % nx).wait_recv()
-    g_own.wait()
+
     ff = w.shape[0]
-    flat_scaled = scaled_all.reshape(NZ * nx * own, ff)
     step = 256
 
-    def turn(k, _):
-        at = pl.multiple_of(k * step, step)
-        scaled_t[:, pl.ds(at, step)] = flat_scaled[pl.ds(at, step), :].T
-        return 0
-
-    lax.fori_loop(0, NZ * nx * own // step, turn, 0)
+    def turn_scaled():
+        remote(scaled_all.at[:, pl.ds(0, nx - 1)], scaled_all.at[:, pl.ds(0, nx - 1)], g_ssem.at[0], g_rsem, me, (q + 1) % nx).wait_recv()
+        g_own.wait()
+        flat_scaled = scaled_all.reshape(NZ * nx * own, ff)
+
+        def turn(k, _):
+            at = pl.multiple_of(k * step, step)
+            scaled_t[:, pl.ds(at, step)] = flat_scaled[pl.ds(at, step), :].T
+            return 0
+
+        lax.fori_loop(0, NZ * nx * own // step, turn, 0)
 
     grp = nx * own
+    planes = [own_first(g) for g in range(NZ)]
 
     def finish(g):
-        dz = plane_order(g)
+        dz = planes[g]
         zz = (z - dz + NZ) % NZ
-        remote(precv.at[dz, pl.ds(0, nx - 1)], precv.at[dz, pl.ds(0, nx - 1)], p_ssem.at[dz], p_rsem.at[dz], me, (q + 1) % nx).wait_recv()
+        landed = precv.at[dz, pl.ds(0, nx - 1)]
+        remote(landed, landed, p_ssem.at[dz], p_rsem.at[dz], me, (q + 1) % nx).wait_recv()
         raw = pf[g % 2, pl.ds(pl.multiple_of(q * own, own), own), :]
         for d in range(1, nx):
             raw = raw + precv[dz, (q + d) % nx].astype(F32)
@@ -261,40 +275,31 @@
             def send():
                 remote(rrow.at[dz], rrecv.at[me], r_ssem, r_rsem, e, q).start()
 
-            if (dy, dc) == (0, 0):
-                pl.when(dz != 0)(send)
-
-                @pl.when(dz == 0)
-                def _():
-                    rrecv[me] = rrow[dz]
+            if (dy, dz, dc) == (0, 0, 0):
+                rrecv[me] = rrow[dz]
             else:
                 send()
-        hg = wcol[dz][:, 0:1] * raw
+        hg = wcol[g][:, 0:1] * raw
         g_gate = hg * up * (sg * (1.0 + gate * (1.0 - sg)))
         g_up = hg * silu
         both = jnp.concatenate([g_gate, g_up], axis=0).astype(BF16)
         pstage[zz] = matmul(join_ref[...], both).astype(BF16).reshape(pstage.shape[1:])
         pltpu.make_async_copy(pstage.at[zz], pre_hbm.at[:, zz], o_sem.at[zz]).start()
 
-    def arrive(g, _):
-        dz = plane_order(g)
-
-        @pl.when(dz != 0)
-        def _():
+    def arrive(g):
+        dz = planes[g]
+        if dz:
             remote(rbuf.at[dz], rbuf.at[dz], d_ssem.at[dz], d_rsem.at[dz], me, (q + 1) % nx).wait_recv()
-
-        @pl.when(dz == 0)
-        def _():
+        else:
             part = rbuf.at[dz, pl.ds(0, (gs - 1) * mr)]
             remote(part, part, d_ssem.at[dz], d_rsem.at[dz], me, (q + 1) % nx).wait_recv()
             block = rbuf.at[dz, pl.ds(pl.multiple_of(slot_me * mr, mr), mr)]
             pltpu.make_async_copy(block, block, d_lsem).wait()
-
-        at = pl.multiple_of(dz * grp, grp)
+        at = g * grp
         for h in range(HALVES):
-            rows[pl.ds(at, grp), h * half : (h + 1) * half] = matmul(order_ref[h], rbuf[dz]).astype(BF16)
+            rows[at : at + grp, h * half : (h + 1) * half] = matmul(order_ref[h], rbuf[dz]).astype(BF16)
         part = lax.dot_general(
-            rows[pl.ds(at, grp), :], w[...], (((1,), (1,)), ((), ())), preferred_element_type=F32
+            rows[at : at + grp, :], w[...], (((1,), (1,)), ((), ())), preferred_element_type=F32
         )
         pf[g % 2] = part
         psend[dz] = part.astype(BF16)
@@ -305,22 +310,41 @@
                 p_ssem.at[dz], p_rsem.at[dz], me, p,
             ).start()
 
-        @pl.when(g > 0)
-        def _():
-            finish(g - 1)
-
-        return 0
-
-    lax.fori_loop(0, NZ, arrive, 0)
-
-    def down_tile(k, _):
-        at = pl.multiple_of(k * step, step)
-        down[:, pl.ds(at, step)] = matmul(scaled_t[...], rows[:, pl.ds(at, step)]).astype(BF16)
-        pltpu.make_async_copy(down.at[:, pl.ds(at, step)], down_hbm.at[:, pl.ds(at, step)], o2_sem.at[k]).start()
-        return 0
-
-    lax.fori_loop(0, width // step, down_tile, 0)
-    finish(NZ - 1)
+    def product(lo, hi, first, last):
+        def tile(k, _):
+            at = pl.ds(pl.multiple_of(k * step, step), step)
+            total = matmul(scaled_t[:, lo * grp : hi * grp], rows[lo * grp : hi * grp, at])
+            if not first:
+                total = total + acc[:, at]
+            if last:
+                down[:, at] = total.astype(BF16)
+                pltpu.make_async_copy(down.at[:, at], down_hbm.at[:, at], o2_sem.at[k]).start()
+            else:
+                acc[:, at] = total
+            return 0
+
+        lax.fori_loop(0, width // step, tile, 0)
+
+    arrive(0)
+    arrive(1)
+    turn_scaled()
+    finish(0)
+    finish(1)
+    arrive(2)
+    arrive(3)
+    product(0, 4, True, False)
+    finish(2)
+    finish(3)
+    arrive(4)
+    arrive(5)
+    product(4, 6, False, False)
+    finish(4)
+    finish(5)
+    arrive(6)
+    arrive(7)
+    product(6, 8, False, True)
+    finish(6)
+    finish(7)
 
     remote(rrecv.at[pl.ds(0, ne - 1)], rrecv.at[pl.ds(0, ne - 1)], r_ssem, r_rsem, me, (q + 1) % nx).wait_recv()
     back = rrecv[...].reshape(ne, 128)
@@ -397,9 +421,10 @@
             pltpu.VMEM((NZ, nx, own, ff), BF16),
             pltpu.VMEM((NZ, 1, 128), F32),
             pltpu.VMEM((ne, 1, 128), F32),
+            pltpu.VMEM((ff, width), F32),
             pltpu.VMEM((ff, width), BF16),
             dma((NZ + 2,)),
-            dma((nx - 1,)), dma,
+            dma((2, nx - 1)), dma((2,)),
             dma((nx - 1,)), dma,
             dma((NZ,)), dma((NZ,)), dma,
             dma, dma,

time: 203 us -> 179 us (0.88)
  Pallas kernels: 193 us -> 170 us
    pallas_call x1, Pallas kernels: 193 us -> 170 us  [local(): pl.pallas_call(functools.partial(kernel, nx, cap), out_shape=[jax.ShapeDt...]
where the time goes in v2:
time: 179 us; the launch traced here: 178 us
  Pallas kernels  170 us (95%)
  local copies, waits for them, and re-layouts  8.31 us (5%)
    pallas_call x1, Pallas kernels, local(): pl.pallas_call(functools.partial(kernel, nx, cap), out_shape=[jax.ShapeDt...  170 us
    unnamed x5, local copies, waits for them, and re-layouts  8.31 us

profile of v2, /device:TPU:1, one launch (start us, length us, event | category | flops | bytes accessed | tf_op | source)
XLA Modules:
  0.0 178.5 jit_solution(12084823081885206499)
XLA Ops:
  0.6 169.5 %shard_map.148 = (bf16[4,8,12,2,1024]{4,3,2,1,0:T(2,128)(2,1)}, bf16[1024,1792]{1,0:T(8,128)(2,1)}, f32[2,128]{1,0:T(2,128)}) custom-call(bf16[128,7168]{1,0:T(8,128)(2,1)} %grad_ref.1, s32[56,128]{1,0:T(8,128)} %bitcast.12, s32[2,128]{1,0:T(2,128)} %bitcast.13, bf16[2,128]{1,0:T(2,128)(2,1)} %bitcast.15, bf16[4,8,12,2,1024]{4,3,2,1,0:T(2,128)(2,1)} %bitcast.10, ...), custom_call_target="tpu_custom_call" | custom-call | tf_op jit(solution)/shard_map/pallas_call | solution.py:392
  170.2 3.6 %copy.19 = bf16[1,1,64,6,2,1024]{5,4,3,2,1,0:T(2,128)(2,1)} copy(bf16[1,1,64,6,2,1024]{5,4,3,2,1,0:T(2,128)(2,1)} %bitcast.11) | data formatting | bytes 3145728
  173.8 0.0 copy-start
  173.8 4.1 %copy.20 = bf16[1,1024,1792]{2,1,0:T(8,128)(2,1)} copy(bf16[1,1024,1792]{2,1,0:T(8,128)(2,1)} %bitcast.9) | data formatting | bytes 7340032
  177.9 0.0 copy-done
  177.9 0.6 copy.21
Async XLA Ops:
  173.8 4.1 %copy-start = (f32[2,128]{1,0:T(2,128)S(1)}, f32[2,128]{1,0:T(2,128)}, u32[]{:S(2)}) copy-start(f32[2,128]{1,0:T(2,128)} %get-tuple-element.8) | copy-start | bytes 3076

commit v3 on v2

--- a/solution.py
+++ b/solution.py
@@ -12,7 +12,7 @@
 F32, BF16, I32 = jnp.float32, jnp.bfloat16, jnp.int32
 NY, NZ, NC = 4, 8, 2
 HALVES = 2
-EARLY = 256
+CUTS = (0, 128, 384)
 
 
 def power_of_two(exponent):
@@ -74,8 +74,6 @@
     width = w.shape[1]
     half = width // HALVES
     blocks = exp_ref.shape[0]
-    inner = [(dy, dc) for dy in range(NY) for dc in range(NC)]
-    slot_me = y * NC + core
 
     def expert_of(dy, dz, dc):
         return ((y + dy) % NY) * (NZ * NC) + ((z + dz) % NZ) * NC + (core + dc) % NC
@@ -85,17 +83,25 @@
             src_ref=src, dst_ref=dst, send_sem=ssem, recv_sem=rsem, device_id=(e, x), device_id_type=MESH
         )
 
-    def far_first(g):
-        return (NZ // 2 + ((g + 1) // 2) * (2 * (g % 2) - 1) + NZ) % NZ
-
-    def own_first(g):
-        return (NZ // 2 * ((g + NZ - 1) // NZ) + (g // 2) * (1 - 2 * (g % 2)) + NZ) % NZ
+    def step_of(k, j):
+        paired = (k + NZ - 2) // NZ
+        far = (1 + ((k + NZ - 2) % NZ) // 2) * (1 - 2 * (j // 2))
+        dz = (1 - paired) * (NZ // 2) * k + paired * (NZ // 2 + far)
+        dy = (1 - paired) * j + paired * (2 * (k % 2) + j % 2)
+        return dy, (dz + NZ) % NZ
+
+    def source(k, j):
+        dy, dz = step_of(k, j)
+        return (y - dy + NY) % NY, (z - dz + NZ) % NZ
 
     w_in = pltpu.make_async_copy(w_hbm, w, in_sem.at[0])
     w_in.start()
-    s_in = [pltpu.make_async_copy(saved_hbm.at[:, j], sv.at[j], in_sem.at[1 + j]) for j in range(NZ)]
-    for c in s_in:
-        c.start()
+
+    def load_saved(n, _):
+        sy, sz = source(n // NY, n % NY)
+        pltpu.make_async_copy(saved_hbm.at[sy, sz], sv.at[n // NY, n % NY], in_sem.at[1]).start()
+        return 0
+
 
     bar = pltpu.get_barrier_semaphore()
     for d in range(1, nx):
@@ -112,7 +118,7 @@
     assigned = a[0] + a[1]
     slot = matmul(assigned.astype(BF16), before_ref[...])
     slot = jnp.where(assigned > 0, slot, -1.0)
-    ksend[...] = slot
+    ksend[...] = slot.astype(BF16)
     combine = comb_ref[...].astype(F32)
     weight = a[0] * combine[0:1, :] + a[1] * combine[1:2, :]
     lane = lax.broadcasted_iota(I32, (ne, 128), 1)
@@ -141,7 +147,7 @@
         p = (q + d) % nx
         k_out.append(remote(ksend, krecv.at[q], k_ssem.at[d - 1], k_rsem, me, p))
         k_out[-1].start()
-    cuts = [slice(0, EARLY), slice(EARLY, half)]
+    cuts = [slice(lo, hi) for lo, hi in zip(CUTS, CUTS[1:] + (half,))]
     for part, cut in enumerate(cuts):
         for d in range(1, nx):
             p = (q + d) % nx
@@ -149,23 +155,22 @@
                 remote(xs.at[p, :, :, cut], tok.at[:, q, :, cut], x_ssem.at[part, d - 1], x_rsem.at[part], me, p)
             )
             x_out[-1].start()
-    x_own = pltpu.make_async_copy(xs.at[q], tok.at[:, q], in_sem.at[NZ + 1])
+    x_own = pltpu.make_async_copy(xs.at[q], tok.at[:, q], in_sem.at[2])
     x_own.start()
     krecv[q] = ksend[...]
+    lax.fori_loop(0, NZ * NY, load_saved, 0)
 
     def send_weight(k, _):
-        dz, rest = k // gs, k % gs
-        dy, dc = rest // NC, rest % NC
+        group, j, dc = k // gs, (k % gs) // NC, k % NC
+        dy, dz = step_of(group, j)
         e = expert_of(dy, dz, dc)
-        remote(wsend.at[e], wrecv.at[dz * gs + slot_me], w_ssem, w_rsem, e, q).start()
+        remote(wsend.at[e], wrecv.at[group * gs + j * NC + core], w_ssem, w_rsem, e, q).start()
         return 0
 
-    lax.fori_loop(1, ne, send_weight, 0)
-    wrecv[slot_me] = wsend[me]
 
     remote(krecv.at[pl.ds(0, nx - 1)], krecv.at[pl.ds(0, nx - 1)], k_ssem.at[0], k_rsem, me, (q + 1) % nx).wait_recv()
     for r in range(nx):
-        s = krecv[r]
+        s = krecv[r].astype(F32)
         for h in range(HALVES):
             at = (h * nx + r) * tokens
             keys[:, at : at + tokens] = jnp.where(s >= 0, s + (h * rc + r * cap), -1.0)
@@ -174,58 +179,65 @@
 
     row_iota = lax.broadcasted_iota(I32, (mr, HALVES * nx * tokens), 0).astype(F32)
 
-    def dispatch(part, order, g, _):
+    own_block = pl.ds(pl.multiple_of(core * mr, mr), mr)
+
+    def dispatch(part, turn, g, _):
         cut = cuts[part]
-        dz = order(g)
-        for i in range(gs):
-            e = (i // NC) * (NZ * NC) + ((z + dz) % NZ) * NC + i % NC
-            hot = jnp.where(row_iota == keys[pl.ds(e, 1), :], 1.0, 0.0).astype(BF16)
-            out = matmul(hot, tok[:, :, :, cut].reshape(HALVES * nx * tokens, cut.stop - cut.start))
-            sbuf[dz, i * mr : (i + 1) * mr, cut] = out.astype(BF16)
-
-        mine = pl.ds(pl.multiple_of(slot_me * mr, mr), mr)
-
-        def send(dy, dc):
-            to = ((y + dy) % NY) * NC + (core + dc) % NC
+        k = (g + turn) % NZ
+        for j in range(NY):
+            dy, dz = step_of(k, j)
+            for c in range(NC):
+                e = (((y + dy) % NY) * NZ + (z + dz) % NZ) * NC + c
+                hot = jnp.where(row_iota == keys[pl.ds(e, 1), :], 1.0, 0.0).astype(BF16)
+                out = matmul(hot, tok[:, :, :, cut].reshape(HALVES * nx * tokens, cut.stop - cut.start))
+                i = j * NC + c
+                sbuf[k, i * mr : (i + 1) * mr, cut] = out.astype(BF16)
+
+        def send(j, dc):
+            dy, dz = step_of(k, j)
+            to = j * NC + (core + dc) % NC
+            at = j * NC + core
             remote(
-                sbuf.at[dz, pl.ds(pl.multiple_of(to * mr, mr), mr), cut], rbuf.at[dz, mine, cut],
-                d_ssem.at[dz], d_rsem.at[dz], expert_of(dy, dz, dc), q,
+                sbuf.at[k, pl.ds(pl.multiple_of(to * mr, mr), mr), cut],
+                rbuf.at[k, pl.ds(pl.multiple_of(at * mr, mr), mr), cut],
+                d_ssem.at[k], d_rsem.at[k], expert_of(dy, dz, dc), q,
             ).start()
 
-        for dy, dc in inner:
-            if (dy, dc) == (0, 0):
-                @pl.when(dz != 0)
-                def _():
-                    send(0, 0)
-
-                @pl.when(dz == 0)
-                def _():
-                    pltpu.make_async_copy(sbuf.at[dz, mine, cut], rbuf.at[dz, mine, cut], d_lsem).start()
-            else:
-                send(dy, dc)
+        for j in range(NY):
+            for dc in range(NC):
+                if (j, dc) == (0, 0):
+                    @pl.when(k != 0)
+                    def _():
+                        send(0, 0)
+
+                    @pl.when(k == 0)
+                    def _():
+                        pltpu.make_async_copy(sbuf.at[k, own_block, cut], rbuf.at[k, own_block, cut], d_lsem).start()
+                else:
+                    send(j, dc)
         return 0
 
-    for part, order in enumerate((far_first, own_first)):
-        cut = cuts[part]
+    for part, cut in enumerate(cuts):
         landed = tok.at[:, pl.ds(0, nx - 1), :, cut]
         remote(landed, landed, x_ssem.at[part, 0], x_rsem.at[part], me, (q + 1) % nx).wait_recv()
-        lax.fori_loop(0, NZ, functools.partial(dispatch, part, order), 0)
-
-    for c in s_in:
-        c.wait()
+        lax.fori_loop(0, NZ, functools.partial(dispatch, part, 0 if part == len(cuts) - 1 else 1), 0)
+        if part == 0:
+            lax.fori_loop(1, ne, send_weight, 0)
+            wrecv[core] = wsend[me]
+
+    pltpu.make_async_copy(sv, sv, in_sem.at[1]).wait()
     remote(wrecv.at[pl.ds(0, ne - 1)], wrecv.at[pl.ds(0, ne - 1)], w_ssem, w_rsem, me, (q + 1) % nx).wait_recv()
 
-    def gate_up(dz):
-        v = sv[(z - dz + NZ) % NZ].reshape(2 * own, w.shape[0])
+    def gate_up(k):
+        v = sv[k].reshape(2 * own, w.shape[0])
         gu = matmul(split_ref[...], v)
         gate, up = gu[:own], gu[own:]
         sg = jax.nn.sigmoid(gate)
         return gate, up, sg, gate * sg
 
     def scale_hidden(g, _):
-        dz = own_first(g)
-        gate, up, sg, silu = gate_up(dz)
-        wr = wrecv[pl.ds(dz * gs, gs)].reshape(gs, 128)
+        gate, up, sg, silu = gate_up(g)
+        wr = wrecv[pl.ds(g * gs, gs)].reshape(gs, 128)
         col = jnp.sum(matmul(repeat_ref[...], wr.astype(BF16)) * pick_ref[...], axis=1, keepdims=True)
         wcol[g] = jnp.broadcast_to(col, (own, 128))
         scaled[g] = (col * (silu * up)).astype(BF16)
@@ -256,58 +268,54 @@
         lax.fori_loop(0, NZ * nx * own // step, turn, 0)
 
     grp = nx * own
-    planes = [own_first(g) for g in range(NZ)]
 
     def finish(g):
-        dz = planes[g]
-        zz = (z - dz + NZ) % NZ
-        landed = precv.at[dz, pl.ds(0, nx - 1)]
-        remote(landed, landed, p_ssem.at[dz], p_rsem.at[dz], me, (q + 1) % nx).wait_recv()
+        landed = precv.at[g, pl.ds(0, nx - 1)]
+        remote(landed, landed, p_ssem.at[g], p_rsem.at[g], me, (q + 1) % nx).wait_recv()
         raw = pf[g % 2, pl.ds(pl.multiple_of(q * own, own), own), :]
         for d in range(1, nx):
-            raw = raw + precv[dz, (q + d) % nx].astype(F32)
-        gate, up, sg, silu = gate_up(dz)
+            raw = raw + precv[g, (q + d) % nx].astype(F32)
+        gate, up, sg, silu = gate_up(g)
         part = jnp.sum(silu * up * raw, axis=1, keepdims=True)
-        rrow[dz] = jnp.sum(part * diag_ref[...], axis=0, keepdims=True)
-        for dy, dc in inner:
-            e = (((y + dy) % NY) * NZ + zz) * NC + (core + dc) % NC
-
-            def send():
-                remote(rrow.at[dz], rrecv.at[me], r_ssem, r_rsem, e, q).start()
-
-            if (dy, dz, dc) == (0, 0, 0):
-                rrecv[me] = rrow[dz]
-            else:
-                send()
+        rrow[g] = jnp.sum(part * diag_ref[...], axis=0, keepdims=True)
+        for j in range(NY):
+            sy, sz = source(g, j)
+            for dc in range(NC):
+                if (g, j, dc) == (0, 0, 0):
+                    rrecv[me] = rrow[g]
+                else:
+                    e = (sy * NZ + sz) * NC + (core + dc) % NC
+                    remote(rrow.at[g], rrecv.at[me], r_ssem, r_rsem, e, q).start()
         hg = wcol[g][:, 0:1] * raw
         g_gate = hg * up * (sg * (1.0 + gate * (1.0 - sg)))
         g_up = hg * silu
         both = jnp.concatenate([g_gate, g_up], axis=0).astype(BF16)
-        pstage[zz] = matmul(join_ref[...], both).astype(BF16).reshape(pstage.shape[1:])
-        pltpu.make_async_copy(pstage.at[zz], pre_hbm.at[:, zz], o_sem.at[zz]).start()
+        pstage[g] = matmul(join_ref[...], both).astype(BF16).reshape(pstage.shape[1:])
+        for j in range(NY):
+            sy, sz = source(g, j)
+            pltpu.make_async_copy(pstage.at[g, j], pre_hbm.at[sy, sz], o_sem.at[g]).start()
 
     def arrive(g):
-        dz = planes[g]
-        if dz:
-            remote(rbuf.at[dz], rbuf.at[dz], d_ssem.at[dz], d_rsem.at[dz], me, (q + 1) % nx).wait_recv()
+        if g:
+            remote(rbuf.at[g], rbuf.at[g], d_ssem.at[g], d_rsem.at[g], me, (q + 1) % nx).wait_recv()
         else:
-            part = rbuf.at[dz, pl.ds(0, (gs - 1) * mr)]
-            remote(part, part, d_ssem.at[dz], d_rsem.at[dz], me, (q + 1) % nx).wait_recv()
-            block = rbuf.at[dz, pl.ds(pl.multiple_of(slot_me * mr, mr), mr)]
+            part = rbuf.at[g, pl.ds(0, (gs - 1) * mr)]
+            remote(part, part, d_ssem.at[g], d_rsem.at[g], me, (q + 1) % nx).wait_recv()
+            block = rbuf.at[g, own_block]
             pltpu.make_async_copy(block, block, d_lsem).wait()
         at = g * grp
         for h in range(HALVES):
-            rows[at : at + grp, h * half : (h + 1) * half] = matmul(order_ref[h], rbuf[dz]).astype(BF16)
+            rows[at : at + grp, h * half : (h + 1) * half] = matmul(order_ref[h], rbuf[g]).astype(BF16)
         part = lax.dot_general(
             rows[at : at + grp, :], w[...], (((1,), (1,)), ((), ())), preferred_element_type=F32
         )
         pf[g % 2] = part
-        psend[dz] = part.astype(BF16)
+        psend[g] = part.astype(BF16)
         for d in range(1, nx):
             p = (q + d) % nx
             remote(
-                psend.at[dz, pl.ds(pl.multiple_of(p * own, own), own)], precv.at[dz, q],
-                p_ssem.at[dz], p_rsem.at[dz], me, p,
+                psend.at[g, pl.ds(pl.multiple_of(p * own, own), own)], precv.at[g, q],
+                p_ssem.at[g], p_rsem.at[g], me, p,
             ).start()
 
     def product(lo, hi, first, last):
@@ -329,29 +337,35 @@
     arrive(1)
     turn_scaled()
     finish(0)
+    arrive(2)
     finish(1)
-    arrive(2)
     arrive(3)
     product(0, 4, True, False)
     finish(2)
+    arrive(4)
     finish(3)
-    arrive(4)
     arrive(5)
     product(4, 6, False, False)
     finish(4)
+    arrive(6)
     finish(5)
-    arrive(6)
     arrive(7)
+    finish(6)
     product(6, 8, False, True)
-    finish(6)
     finish(7)
 
     remote(rrecv.at[pl.ds(0, ne - 1)], rrecv.at[pl.ds(0, ne - 1)], r_ssem, r_rsem, me, (q + 1) % nx).wait_recv()
     back = rrecv[...].reshape(ne, 128)
     value = jnp.zeros((ne, tokens), F32)
+    slot = ksend[...].astype(F32)
+    expert = lax.broadcasted_iota(I32, (ne, 128), 0)
+    dy = (expert // (NZ * NC) - y + NY) % NY
+    dz = ((expert // NC) % NZ - z + NZ) % NZ
+    j = jnp.where(dz % (NZ // 2) == 0, dy, dy % 2 + jnp.where(dz < NZ // 2, 2, 0))
+    place = (j * NC + core) * cap
     for c in range(cap):
-        column = jnp.sum(jnp.where(lane == slot_me * cap + c, back, 0.0), axis=1, keepdims=True)
-        value = jnp.where(ksend[...] == c, column, value)
+        column = jnp.sum(jnp.where(lane == place + c, back, 0.0), axis=1, keepdims=True)
+        value = jnp.where(slot == c, column, value)
     for k in range(2):
         mine = jnp.where(expert_iota == ids_ref[k : k + 1, :], value, 0.0)
         router_ref[k : k + 1, :] = jnp.sum(mine, axis=0, keepdims=True)
@@ -372,6 +386,27 @@
         pltpu.make_async_copy(
             down.at[:, k * step : (k + 1) * step], down_hbm.at[:, k * step : (k + 1) * step], o2_sem.at[k]
         ).wait()
+
+
+def hand_over(pieces, pre_in, down_in, router_in, pre_out, down_out, router_out, pre_buf, down_buf, in_sem, out_sem):
+    parts = []
+    rows = down_buf.shape[0] // pieces
+    for j in range(pieces):
+        at = pl.ds(j * rows, rows)
+        parts.append((down_in.at[at], down_buf.at[at], down_out.at[at]))
+    for j in range(pre_buf.shape[0]):
+        for i in range(pre_buf.shape[1]):
+            parts.append((pre_in.at[j, i], pre_buf.at[j, i], pre_out.at[j, i]))
+    loads = [pltpu.make_async_copy(a, b, in_sem.at[n]) for n, (a, b, _) in enumerate(parts)]
+    stores = [pltpu.make_async_copy(b, c, out_sem.at[n]) for n, (_, b, c) in enumerate(parts)]
+    for c in loads:
+        c.start()
+    router_out[...] = router_in[...]
+    for load, store in zip(loads, stores):
+        load.wait()
+        store.start()
+    for c in stores:
+        c.wait()
 
 
 def local(grad_out, grad_exponent, expert_ids, combine, saved_acts, w_down):
@@ -401,8 +436,8 @@
         scratch_shapes=[
             pltpu.VMEM((nx, HALVES, tokens, half), BF16),
             pltpu.VMEM((HALVES, nx, tokens, half), BF16),
-            pltpu.VMEM((ne, tokens), F32),
-            pltpu.VMEM((nx, ne, tokens), F32),
+            pltpu.VMEM((ne, tokens), BF16),
+            pltpu.VMEM((nx, ne, tokens), BF16),
             pltpu.VMEM((ne, HALVES * nx * tokens), F32),
             pltpu.VMEM((NZ, gs * mr, half), BF16),
             pltpu.VMEM((NZ, gs * mr, half), BF16),
@@ -423,8 +458,8 @@
             pltpu.VMEM((ne, 1, 128), F32),
             pltpu.VMEM((ff, width), F32),
             pltpu.VMEM((ff, width), BF16),
-            dma((NZ + 2,)),
-            dma((2, nx - 1)), dma((2,)),
+            dma((3,)),
+            dma((len(CUTS), nx - 1)), dma((len(CUTS),)),
             dma((nx - 1,)), dma,
             dma((NZ,)), dma((NZ,)), dma,
             dma, dma,
@@ -437,6 +472,16 @@
             collective_id=0, has_side_effects=True, vmem_limit_bytes=60 << 20
         ),
     )(grad_out, grad_exponent.T, expert_ids.T, combine.T, saved, w_down[0], *consts)
+    pieces = 16
+    pre, down, router = pl.pallas_call(
+        functools.partial(hand_over, pieces),
+        out_shape=[jax.ShapeDtypeStruct(v.shape, v.dtype) for v in (pre, down, router)],
+        in_specs=[hbm, hbm, vmem],
+        out_specs=[hbm, hbm, vmem],
+        scratch_shapes=[
+            pltpu.VMEM(pre.shape, BF16), pltpu.VMEM(down.shape, BF16), dma((pieces + NY * NZ,)), dma((pieces + NY * NZ,)),
+        ],
+    )(pre, down, router)
     return pre.reshape(saved_acts.shape), down[None], router.T
 
 

time: 179 us -> 168 us (0.939)
  local copies, waits for them, and re-layouts: 8.31 us -> 0 us
  Pallas kernels: 170 us -> 167 us
    pallas_call x1, Pallas kernels: 170 us -> 160 us  [local(): pl.pallas_call(functools.partial(kernel, nx, cap), out_shape=[jax.ShapeDt...]
    unnamed x5 -> x0, local copies, waits for them, and re-layouts: 8.31 us -> none
    pallas_call x0 -> x1, Pallas kernels: none -> 6.65 us  [local(): pl.pallas_call(functools.partial(hand_over, pieces), out_shape=[jax.Shape...]
where the time goes in v3:
time: 168 us
  Pallas kernels  167 us (99%)
    pallas_call x1, Pallas kernels, local(): pl.pallas_call(functools.partial(kernel, nx, cap), out_shape=[jax.ShapeDt...  160 us
    pallas_call x1, Pallas kernels, local(): pl.pallas_call(functools.partial(hand_over, pieces), out_shape=[jax.Shape...  6.65 us

profile of v3, /device:TPU:1, one launch (start us, length us, event | category | flops | bytes accessed | tf_op | source)
XLA Modules:
  0.0 167.8 jit_solution(4733722086872239494)
XLA Ops:
  0.6 160.3 %shard_map.148 = (bf16[4,8,12,2,1024]{4,3,2,1,0:T(2,128)(2,1)}, bf16[1024,1792]{1,0:T(8,128)(2,1)}, f32[2,128]{1,0:T(2,128)}) custom-call(bf16[128,7168]{1,0:T(8,128)(2,1)} %grad_ref.1, s32[56,128]{1,0:T(8,128)} %bitcast.10, s32[2,128]{1,0:T(2,128)} %bitcast.11, bf16[2,128]{1,0:T(2,128)(2,1)} %bitcast.12, bf16[4,8,12,2,1024]{4,3,2,1,0:T(2,128)(2,1)} %bitcast.9, ...), custom_call_target="tpu_custom_call" | custom-call | tf_op jit(solution)/shard_map/pallas_call | solution.py:427
  161.0 6.7 %shard_map.149 = (bf16[4,8,12,2,1024]{4,3,2,1,0:T(2,128)(2,1)}, bf16[1024,1792]{1,0:T(8,128)(2,1)}, f32[2,128]{1,0:T(2,128)}) custom-call(bf16[4,8,12,2,1024]{4,3,2,1,0:T(2,128)(2,1)} %get-tuple-element.9.pre_in, bf16[1024,1792]{1,0:T(8,128)(2,1)} %get-tuple-element.10.down_in, f32[2,128]{1,0:T(2,128)} %get-tuple-element.11.router_in), custom_call_target="tpu_custom_call" | custom-call | tf_op jit(solution)/shard_map/pallas_call | solution.py:476

commit v4 on v3

--- a/solution.py
+++ b/solution.py
@@ -57,9 +57,9 @@
     grad_ref, exp_ref, ids_ref, comb_ref, saved_hbm, w_hbm,
     order_ref, split_ref, join_ref, repeat_ref, pick_ref, diag_ref, before_ref,
     pre_hbm, down_hbm, router_ref,
-    xs, tok, ksend, krecv, keys, sbuf, rbuf, rows, w, sv, pstage, wsend, wrecv, wcol,
+    xs, tok, tok_near, ksend, krecv, k_near, keys, sbuf, rbuf, rows, w, sv, pstage, wsend, wrecv, wcol,
     scaled, scaled_all, scaled_t, pf, psend, precv, rrow, rrecv, acc, down,
-    in_sem, x_ssem, x_rsem, k_ssem, k_rsem, d_ssem, d_rsem, d_lsem, w_ssem, w_rsem,
+    in_sem, x_ssem, x_rsem, k_ssem, k_rsem, n_ssem, n_rsem, kn_ssem, kn_rsem, d_ssem, d_rsem, d_lsem, w_ssem, w_rsem,
     g_ssem, g_rsem, g_lsem, p_ssem, p_rsem, r_ssem, r_rsem, o_sem, o2_sem,
 ):
     me = lax.axis_index("expert")
@@ -169,61 +169,124 @@
 
 
     remote(krecv.at[pl.ds(0, nx - 1)], krecv.at[pl.ds(0, nx - 1)], k_ssem.at[0], k_rsem, me, (q + 1) % nx).wait_recv()
-    for r in range(nx):
-        s = krecv[r].astype(F32)
-        for h in range(HALVES):
-            at = (h * nx + r) * tokens
-            keys[:, at : at + tokens] = jnp.where(s >= 0, s + (h * rc + r * cap), -1.0)
-
+    near = [((z + NZ - 1) % NZ, (z + 1) % NZ), ((z + 1) % NZ, (z + NZ - 1) % NZ)]
+
+    def device_at(plane):
+        return (y * NZ + plane) * NC + core
+
+    kn_out = [
+        remote(krecv, k_near.at[i], kn_ssem.at[i], kn_rsem.at[i], device_at(near[i][0]), q) for i in range(2)
+    ]
+    for c in kn_out:
+        c.start()
+
+    def make_keys(i, tables):
+        for r in range(nx):
+            s = tables[r].astype(F32)
+            for h in range(HALVES):
+                at = (h * nx + r) * tokens
+                keys[i, :, at : at + tokens] = jnp.where(s >= 0, s + (h * rc + r * cap), -1.0)
+
+    make_keys(2, krecv)
     x_own.wait()
 
     row_iota = lax.broadcasted_iota(I32, (mr, HALVES * nx * tokens), 0).astype(F32)
 
-    own_block = pl.ds(pl.multiple_of(core * mr, mr), mr)
-
-    def dispatch(part, turn, g, _):
+    def build(k, j, cut, held, i, plane):
+        dy, dz = step_of(k, j)
+        for c in range(NC):
+            e = (((y + dy) % NY) * NZ + (plane + dz) % NZ) * NC + c
+            hot = jnp.where(row_iota == keys[i, pl.ds(e, 1), :], 1.0, 0.0).astype(BF16)
+            out = matmul(hot, held.reshape(HALVES * nx * tokens, cut.stop - cut.start))
+            at = (j * NC + c) * mr
+            sbuf[k, at : at + mr, cut] = out.astype(BF16)
+
+    def ends(k, j, dc, cut):
+        to, at = j * NC + (core + dc) % NC, j * NC + core
+        return (
+            sbuf.at[k, pl.ds(pl.multiple_of(to * mr, mr), mr), cut],
+            rbuf.at[k, pl.ds(pl.multiple_of(at * mr, mr), mr), cut],
+        )
+
+    def send(k, j, dc, cut, plane):
+        dy, dz = step_of(k, j)
+        e = (((y + dy) % NY) * NZ + (plane + dz) % NZ) * NC + (core + dc) % NC
+        src, dst = ends(k, j, dc, cut)
+        remote(src, dst, d_ssem.at[k], d_rsem.at[k], e, q).start()
+
+    def dispatch_own(part):
         cut = cuts[part]
-        k = (g + turn) % NZ
         for j in range(NY):
-            dy, dz = step_of(k, j)
-            for c in range(NC):
-                e = (((y + dy) % NY) * NZ + (z + dz) % NZ) * NC + c
-                hot = jnp.where(row_iota == keys[pl.ds(e, 1), :], 1.0, 0.0).astype(BF16)
-                out = matmul(hot, tok[:, :, :, cut].reshape(HALVES * nx * tokens, cut.stop - cut.start))
-                i = j * NC + c
-                sbuf[k, i * mr : (i + 1) * mr, cut] = out.astype(BF16)
-
-        def send(j, dc):
-            dy, dz = step_of(k, j)
-            to = j * NC + (core + dc) % NC
-            at = j * NC + core
-            remote(
-                sbuf.at[k, pl.ds(pl.multiple_of(to * mr, mr), mr), cut],
-                rbuf.at[k, pl.ds(pl.multiple_of(at * mr, mr), mr), cut],
-                d_ssem.at[k], d_rsem.at[k], expert_of(dy, dz, dc), q,
-            ).start()
-
+            build(0, j, cut, tok[:, :, :, cut], 2, z)
         for j in range(NY):
             for dc in range(NC):
                 if (j, dc) == (0, 0):
-                    @pl.when(k != 0)
+                    src, dst = ends(0, 0, 0, cut)
+                    pltpu.make_async_copy(src, dst, d_lsem.at[0]).start()
+                else:
+                    send(0, j, dc, cut, z)
+
+    def dispatch(part, g, _):
+        cut = cuts[part]
+        later, last = (g + NZ - 2) // (NZ - 1), (g + NZ - 4) // (NZ - 1)
+        k = 1 + later * (1 - last) * (g + NZ - 4) + last * (g - 2)
+        for j in range(NY):
+            i = j // 2
+            build(k, j, cut, tok_near[i, :, :, :, cut], i, near[i][1])
+        for j in range(NY):
+            plane = near[j // 2][1]
+            for dc in range(NC):
+                if (j % 2, dc) == (0, 0):
+                    @pl.when(k != NZ - 2)
                     def _():
-                        send(0, 0)
-
-                    @pl.when(k == 0)
+                        send(k, j, 0, cut, plane)
+
+                    @pl.when(k == NZ - 2)
                     def _():
-                        pltpu.make_async_copy(sbuf.at[k, own_block, cut], rbuf.at[k, own_block, cut], d_lsem).start()
+                        src, dst = ends(k, j, 0, cut)
+                        pltpu.make_async_copy(src, dst, d_lsem.at[1]).start()
                 else:
-                    send(j, dc)
+                    send(k, j, dc, cut, plane)
         return 0
 
-    for part, cut in enumerate(cuts):
+    n_out = []
+
+    def pass_on(part):
+        cut = cuts[part]
         landed = tok.at[:, pl.ds(0, nx - 1), :, cut]
         remote(landed, landed, x_ssem.at[part, 0], x_rsem.at[part], me, (q + 1) % nx).wait_recv()
-        lax.fori_loop(0, NZ, functools.partial(dispatch, part, 0 if part == len(cuts) - 1 else 1), 0)
-        if part == 0:
-            lax.fori_loop(1, ne, send_weight, 0)
-            wrecv[core] = wsend[me]
+        for i in range(2):
+            n_out.append(
+                remote(
+                    tok.at[:, :, :, cut], tok_near.at[i, :, :, :, cut],
+                    n_ssem.at[part, i], n_rsem.at[part, i], device_at(near[i][0]), q,
+                )
+            )
+            n_out[-1].start()
+
+    def await_near(part):
+        for i in range(2):
+            landed = tok_near.at[i, :, :, :, cuts[part]]
+            remote(landed, landed, n_ssem.at[part, i], n_rsem.at[part, i], me, (q + 1) % nx).wait_recv()
+
+    def forward(part):
+        lax.fori_loop(0, NZ - 1, functools.partial(dispatch, part), 0)
+
+    pass_on(0)
+    dispatch_own(0)
+    for i in range(2):
+        remote(k_near.at[i], k_near.at[i], kn_ssem.at[i], kn_rsem.at[i], me, (q + 1) % nx).wait_recv()
+        make_keys(i, k_near.at[i])
+    pass_on(1)
+    await_near(0)
+    forward(0)
+    lax.fori_loop(1, ne, send_weight, 0)
+    wrecv[core] = wsend[me]
+    pass_on(2)
+    dispatch_own(1)
+    await_near(1)
+    forward(1)
+    dispatch_own(2)
 
     pltpu.make_async_copy(sv, sv, in_sem.at[1]).wait()
     remote(wrecv.at[pl.ds(0, ne - 1)], wrecv.at[pl.ds(0, ne - 1)], w_ssem, w_rsem, me, (q + 1) % nx).wait_recv()
@@ -250,6 +313,8 @@
         g_out[-1].start()
     g_own = pltpu.make_async_copy(scaled, scaled_all.at[:, q], g_lsem)
     g_own.start()
+    await_near(2)
+    forward(2)
     w_in.wait()
 
     ff = w.shape[0]
@@ -268,11 +333,13 @@
         lax.fori_loop(0, NZ * nx * own // step, turn, 0)
 
     grp = nx * own
+    taken = [0, 6, 7, 1, 2, 3, 4, 5]
+    stay = [1] + [0] * (NZ - 3) + [2, 0]
 
     def finish(g):
         landed = precv.at[g, pl.ds(0, nx - 1)]
         remote(landed, landed, p_ssem.at[g], p_rsem.at[g], me, (q + 1) % nx).wait_recv()
-        raw = pf[g % 2, pl.ds(pl.multiple_of(q * own, own), own), :]
+        raw = pf[taken.index(g) % 2, pl.ds(pl.multiple_of(q * own, own), own), :]
         for d in range(1, nx):
             raw = raw + precv[g, (q + d) % nx].astype(F32)
         gate, up, sg, silu = gate_up(g)
@@ -296,20 +363,18 @@
             pltpu.make_async_copy(pstage.at[g, j], pre_hbm.at[sy, sz], o_sem.at[g]).start()
 
     def arrive(g):
-        if g:
-            remote(rbuf.at[g], rbuf.at[g], d_ssem.at[g], d_rsem.at[g], me, (q + 1) % nx).wait_recv()
-        else:
-            part = rbuf.at[g, pl.ds(0, (gs - 1) * mr)]
-            remote(part, part, d_ssem.at[g], d_rsem.at[g], me, (q + 1) % nx).wait_recv()
-            block = rbuf.at[g, own_block]
-            pltpu.make_async_copy(block, block, d_lsem).wait()
+        part = rbuf.at[g, pl.ds(0, (gs - stay[g]) * mr)]
+        remote(part, part, d_ssem.at[g], d_rsem.at[g], me, (q + 1) % nx).wait_recv()
+        if stay[g]:
+            block = rbuf.at[g, pl.ds(0, stay[g] * mr)]
+            pltpu.make_async_copy(block, block, d_lsem.at[stay[g] - 1]).wait()
         at = g * grp
         for h in range(HALVES):
             rows[at : at + grp, h * half : (h + 1) * half] = matmul(order_ref[h], rbuf[g]).astype(BF16)
         part = lax.dot_general(
             rows[at : at + grp, :], w[...], (((1,), (1,)), ((), ())), preferred_element_type=F32
         )
-        pf[g % 2] = part
+        pf[taken.index(g) % 2] = part
         psend[g] = part.astype(BF16)
         for d in range(1, nx):
             p = (q + d) % nx
@@ -334,25 +399,26 @@
         lax.fori_loop(0, width // step, tile, 0)
 
     arrive(0)
+    arrive(6)
+    finish(0)
+    arrive(7)
+    finish(6)
+    turn_scaled()
+    product(6, 8, True, False)
+    finish(7)
     arrive(1)
-    turn_scaled()
-    finish(0)
+    product(0, 2, False, False)
     arrive(2)
     finish(1)
     arrive(3)
-    product(0, 4, True, False)
     finish(2)
+    product(2, 4, False, False)
     arrive(4)
     finish(3)
     arrive(5)
-    product(4, 6, False, False)
     finish(4)
-    arrive(6)
+    product(4, 6, False, True)
     finish(5)
-    arrive(7)
-    finish(6)
-    product(6, 8, False, True)
-    finish(7)
 
     remote(rrecv.at[pl.ds(0, ne - 1)], rrecv.at[pl.ds(0, ne - 1)], r_ssem, r_rsem, me, (q + 1) % nx).wait_recv()
     back = rrecv[...].reshape(ne, 128)
@@ -370,14 +436,14 @@
         mine = jnp.where(expert_iota == ids_ref[k : k + 1, :], value, 0.0)
         router_ref[k : k + 1, :] = jnp.sum(mine, axis=0, keepdims=True)
 
-    for c in k_out + x_out + g_out:
+    for c in k_out + kn_out + x_out + n_out + g_out:
         c.wait_send()
     part = wsend.at[pl.ds(0, ne - 1)]
     remote(part, part, w_ssem, w_rsem, me, (q + 1) % nx).wait_send()
     part = rrecv.at[pl.ds(0, ne - 1)]
     remote(part, part, r_ssem, r_rsem, me, (q + 1) % nx).wait_send()
     for j in range(NZ):
-        part = sbuf.at[j] if j else sbuf.at[j, pl.ds(0, (gs - 1) * mr)]
+        part = sbuf.at[j, pl.ds(0, (gs - stay[j]) * mr)]
         remote(part, part, d_ssem.at[j], d_rsem.at[j], me, (q + 1) % nx).wait_send()
         part = psend.at[j, pl.ds(0, (nx - 1) * own)]
         remote(part, part, p_ssem.at[j], p_rsem.at[j], me, (q + 1) % nx).wait_send()
@@ -436,9 +502,11 @@
         scratch_shapes=[
             pltpu.VMEM((nx, HALVES, tokens, half), BF16),
             pltpu.VMEM((HALVES, nx, tokens, half), BF16),
+            pltpu.VMEM((2, HALVES, nx, tokens, half), BF16),
             pltpu.VMEM((ne, tokens), BF16),
             pltpu.VMEM((nx, ne, tokens), BF16),
-            pltpu.VMEM((ne, HALVES * nx * tokens), F32),
+            pltpu.VMEM((2, nx, ne, tokens), BF16),
+            pltpu.VMEM((3, ne, HALVES * nx * tokens), F32),
             pltpu.VMEM((NZ, gs * mr, half), BF16),
             pltpu.VMEM((NZ, gs * mr, half), BF16),
             pltpu.VMEM((NZ * nx * own, width), BF16),
@@ -461,7 +529,9 @@
             dma((3,)),
             dma((len(CUTS), nx - 1)), dma((len(CUTS),)),
             dma((nx - 1,)), dma,
-            dma((NZ,)), dma((NZ,)), dma,
+            dma((len(CUTS), 2)), dma((len(CUTS), 2)),
+            dma((2,)), dma((2,)),
+            dma((NZ,)), dma((NZ,)), dma((2,)),
             dma, dma,
             dma((nx - 1,)), dma, dma,
             dma((NZ,)), dma((NZ,)),

time: 168 us -> 155 us (0.923)
  Pallas kernels: 167 us -> 154 us
    pallas_call x1, Pallas kernels: 160 us -> 147 us  [local(): pl.pallas_call(functools.partial(kernel, nx, cap), out_shape=[jax.ShapeDt...]
where the time goes in v4:
time: 155 us
  Pallas kernels  154 us (99%)
    pallas_call x1, Pallas kernels, local(): pl.pallas_call(functools.partial(kernel, nx, cap), out_shape=[jax.ShapeDt...  147 us
    pallas_call x1, Pallas kernels, local(): pl.pallas_call(functools.partial(hand_over, pieces), out_shape=[jax.Shape...  6.65 us

profile of v4, /device:TPU:1, one launch (start us, length us, event | category | flops | bytes accessed | tf_op | source)
XLA Modules:
  0.0 154.7 jit_solution(3594937008664347792)
XLA Ops:
  0.6 147.3 %shard_map.148 = (bf16[4,8,12,2,1024]{4,3,2,1,0:T(2,128)(2,1)}, bf16[1024,1792]{1,0:T(8,128)(2,1)}, f32[2,128]{1,0:T(2,128)}) custom-call(bf16[128,7168]{1,0:T(8,128)(2,1)} %grad_ref.1, s32[56,128]{1,0:T(8,128)} %bitcast.10, s32[2,128]{1,0:T(2,128)} %bitcast.11, bf16[2,128]{1,0:T(2,128)(2,1)} %bitcast.12, bf16[4,8,12,2,1024]{4,3,2,1,0:T(2,128)(2,1)} %bitcast.9, ...), custom_call_target="tpu_custom_call" | custom-call | tf_op jit(solution)/shard_map/pallas_call | solution.py:493
  147.9 6.7 %shard_map.149 = (bf16[4,8,12,2,1024]{4,3,2,1,0:T(2,128)(2,1)}, bf16[1024,1792]{1,0:T(8,128)(2,1)}, f32[2,128]{1,0:T(2,128)}) custom-call(bf16[4,8,12,2,1024]{4,3,2,1,0:T(2,128)(2,1)} %get-tuple-element.9.pre_in, bf16[1024,1792]{1,0:T(8,128)(2,1)} %get-tuple-element.10.down_in, f32[2,128]{1,0:T(2,128)} %get-tuple-element.11.router_in), custom_call_target="tpu_custom_call" | custom-call | tf_op jit(solution)/shard_map/pallas_call | solution.py:546

commit v5 on v4

--- a/solution.py
+++ b/solution.py
@@ -412,12 +412,11 @@
     finish(1)
     arrive(3)
     finish(2)
-    product(2, 4, False, False)
     arrive(4)
     finish(3)
     arrive(5)
+    product(2, 6, False, True)
     finish(4)
-    product(4, 6, False, True)
     finish(5)
 
     remote(rrecv.at[pl.ds(0, ne - 1)], rrecv.at[pl.ds(0, ne - 1)], r_ssem, r_rsem, me, (q + 1) % nx).wait_recv()
@@ -461,8 +460,7 @@
         at = pl.ds(j * rows, rows)
         parts.append((down_in.at[at], down_buf.at[at], down_out.at[at]))
     for j in range(pre_buf.shape[0]):
-        for i in range(pre_buf.shape[1]):
-            parts.append((pre_in.at[j, i], pre_buf.at[j, i], pre_out.at[j, i]))
+        parts.append((pre_in.at[j], pre_buf.at[j], pre_out.at[j]))
     loads = [pltpu.make_async_copy(a, b, in_sem.at[n]) for n, (a, b, _) in enumerate(parts)]
     stores = [pltpu.make_async_copy(b, c, out_sem.at[n]) for n, (_, b, c) in enumerate(parts)]
     for c in loads:
@@ -542,14 +540,14 @@
             collective_id=0, has_side_effects=True, vmem_limit_bytes=60 << 20
         ),
     )(grad_out, grad_exponent.T, expert_ids.T, combine.T, saved, w_down[0], *consts)
-    pieces = 16
+    pieces = 4
     pre, down, router = pl.pallas_call(
         functools.partial(hand_over, pieces),
         out_shape=[jax.ShapeDtypeStruct(v.shape, v.dtype) for v in (pre, down, router)],
         in_specs=[hbm, hbm, vmem],
         out_specs=[hbm, hbm, vmem],
         scratch_shapes=[
-            pltpu.VMEM(pre.shape, BF16), pltpu.VMEM(down.shape, BF16), dma((pieces + NY * NZ,)), dma((pieces + NY * NZ,)),
+            pltpu.VMEM(pre.shape, BF16), pltpu.VMEM(down.shape, BF16), dma((pieces + NY,)), dma((pieces + NY,)),
         ],
     )(pre, down, router)
     return pre.reshape(saved_acts.shape), down[None], router.T

time: 155 us -> 154 us (level)
  no operation moved by 1% of the time
where the time goes in v5:
time: 154 us; the launch traced here: 153 us
  Pallas kernels  153 us (99%)
    pallas_call x1, Pallas kernels, local(): pl.pallas_call(functools.partial(kernel, nx, cap), out_shape=[jax.ShapeDt...  147 us
    pallas_call x1, Pallas kernels, local(): pl.pallas_call(functools.partial(hand_over, pieces), out_shape=[jax.Shape...  5.52 us

profile of v5, /device:TPU:1, one launch (start us, length us, event | category | flops | bytes accessed | tf_op | source)
XLA Modules:
  0.0 153.4 jit_solution(7841901424303192397)
XLA Ops:
  0.6 147.1 %shard_map.148 = (bf16[4,8,12,2,1024]{4,3,2,1,0:T(2,128)(2,1)}, bf16[1024,1792]{1,0:T(8,128)(2,1)}, f32[2,128]{1,0:T(2,128)}) custom-call(bf16[128,7168]{1,0:T(8,128)(2,1)} %grad_ref.1, s32[56,128]{1,0:T(8,128)} %bitcast.10, s32[2,128]{1,0:T(2,128)} %bitcast.11, bf16[2,128]{1,0:T(2,128)(2,1)} %bitcast.12, bf16[4,8,12,2,1024]{4,3,2,1,0:T(2,128)(2,1)} %bitcast.9, ...), custom_call_target="tpu_custom_call" | custom-call | tf_op jit(solution)/shard_map/pallas_call | solution.py:491
  147.7 5.5 %shard_map.149 = (bf16[4,8,12,2,1024]{4,3,2,1,0:T(2,128)(2,1)}, bf16[1024,1792]{1,0:T(8,128)(2,1)}, f32[2,128]{1,0:T(2,128)}) custom-call(bf16[4,8,12,2,1024]{4,3,2,1,0:T(2,128)(2,1)} %get-tuple-element.9.pre_in, bf16[1024,1792]{1,0:T(8,128)(2,1)} %get-tuple-element.10.down_in, f32[2,128]{1,0:T(2,128)} %get-tuple-element.11.router_in), custom_call_target="tpu_custom_call" | custom-call | tf_op jit(solution)/shard_map/pallas_call | solution.py:544
